TPU v7x, 32 devices: a whole 2x2x4 slice. The times are simulated.
32 devices in a mesh: patch: 4 (over z), mode: 8 (over y, x, core).
Axes of the slice: x: 2, y: 2, z: 4, core: 2. Of those that a mesh axis runs over, the one named last changes fastest.
Arguments:
- sky_map: bfloat16 [32, 8192, 64], P('patch', 'mode'), may hold values from -6 to 6
- pixel_mask: int32 [32, 8192], P('patch', 'mode'), may hold values 0 or 1
- noise_factor: float32 [32, 8, 64, 64], P('patch', 'mode'), as said below
- cycle_legendre: float32 [32, 6144, 4], P('patch', 'mode'), may hold values from -6 to 6
- band_power: float32 [6144, 4], P('mode', 'patch'), may hold values from 0.1 to 10
- channel_cov: float32 [64, 64], replicated
- test_matrix: bfloat16 [4, 6144, 2, 512], P('patch', 'mode'), may hold values from -6 to 6
Outputs:
- sketch: float32 [64, 512], P(None, ('patch', 'mode'))
Inputs may be any that keep to these rules, and one draw needn't show every extreme that they name: `noise_factor`: each noise factor is lower triangular with a positive diagonal.
All inputs are finite; a program needn't handle non-finite values. No bound on the sum of `pixel_mask` on one device may be relied on, other than what follows from the above.
Results may differ from a plain program's by a relative error of at most 0.017.
Values may be sent and summed in bfloat16 or wider, within the bound.
No kernel may reach another device: no remote copies, remote signals or barrier semaphores. Data moves between devices by JAX's collectives and lax.ppermute only.
A program may use at most 64 MiB of HBM per device.

v0:
```python
import math

import jax
import jax.numpy as jnp
from jax import lax
from jax.sharding import PartitionSpec as P


def tables(mode_start, mode_rows, pixel_rows, cycle_pixels):
    modes = mode_start + lax.iota(jnp.int32, mode_rows)
    pixels = lax.iota(jnp.int32, pixel_rows)
    phase = modes[:, None] * pixels[None, :] % cycle_pixels
    angle = phase.astype(jnp.float32) * (2.0 * math.pi / cycle_pixels)
    return (jnp.cos(angle).astype(jnp.bfloat16), jnp.sin(angle).astype(jnp.bfloat16))


def fourier(mode_start, mode_rows, values, cycle_pixels):
    cosine, sine = tables(mode_start, mode_rows, values.shape[0], cycle_pixels)
    real_part = jnp.dot(cosine, values, preferred_element_type=jnp.float32)
    imag_part = -jnp.dot(sine, values, preferred_element_type=jnp.float32)
    return jnp.concatenate([real_part, imag_part], axis=1)


def local(sky_map, pixel_mask, noise_factor, cycle_legendre, band_power, channel_cov, test_matrix):
    cycle_count, pixel_count, chans = sky_map.shape
    mode_count, offset_count = band_power.shape
    mode_devices = lax.axis_size("mode")
    cycle_pixels = pixel_count * mode_devices
    white = jnp.einsum(
        "rdc,rjc->rjd",
        noise_factor[:, 0],
        sky_map.astype(jnp.float32),
        precision=lax.Precision.HIGHEST,
    )
    whitened = (white * pixel_mask.astype(jnp.float32)[:, :, None]).astype(jnp.bfloat16)
    by_pixel = jnp.transpose(whitened, (1, 0, 2))
    flat_pixels = by_pixel.reshape(pixel_count, cycle_count * chans)
    mode_start = lax.axis_index("mode") * mode_count
    four = fourier(
        mode_start,
        mode_count,
        lax.all_gather(flat_pixels, "mode", axis=0, tiled=True),
        cycle_pixels,
    )
    four = four.reshape(mode_count, 2, cycle_count, chans)
    alm = lax.psum_scatter(
        jnp.einsum("rmk,mtrc->kmtc", cycle_legendre, four, precision=lax.Precision.HIGHEST).astype(
            jnp.bfloat16
        ),
        "patch",
        scatter_dimension=0,
        tiled=True,
    ).astype(jnp.float32)
    mixed = jnp.einsum("dc,kmtc->kmtd", channel_cov, alm, precision=lax.Precision.HIGHEST)
    scaled = (mixed * jnp.transpose(band_power)[:, :, None, None]).astype(jnp.bfloat16)
    left = scaled.reshape(-1, chans)
    right = test_matrix.reshape(-1, test_matrix.shape[3])
    partial_sketch = jnp.einsum("pc,ps->cs", left, right, preferred_element_type=jnp.float32)
    return lax.psum_scatter(partial_sketch, ("patch", "mode"), scatter_dimension=1, tiled=True)


def solution(mesh):
    return jax.shard_map(
        local,
        mesh=mesh,
        in_specs=(
            P("patch", "mode", None),
            P("patch", "mode"),
            P("patch", "mode", None, None),
            P("patch", "mode", None),
            P("mode", "patch"),
            P(),
            P("patch", "mode", None, None),
        ),
        out_specs=P(None, ("patch", "mode")),
        check_vma=False,
    )
```

profile of v0, /device:TPU:0, one launch (start us, length us, event | category | flops | bytes accessed | tf_op | source)
XLA Modules:
  0.0 410.8 jit_solution(14754352062783721086)
XLA Ops:
  6.5 0.0 copy-start
  6.5 0.0 all-gather.2.cloned.1.call-start
  6.5 0.9 convert_bitcast_fusion
  7.4 3.2 fusion.10
  10.7 0.0 all-gather.2.cloned.1.call-update
  10.7 0.0 reduce-scatter.3.cloned.1.call-start
  10.7 1.5 copy.19
  12.2 95.2 %sine_convert_fusion.6 = bf16[768,8192]{1,0:T(8,128)(2,1)} fusion(s32[768]{0:T(1024)S(1)} %iota_add_fusion), kind=kLoop, calls=%fused_computation.6.clone.clone.clone.clone.1 | loop fusion | flops 94371840 | bytes 12585984 | tf_op jit(solution)/shard_map/dot_general | solution.py:20
  107.5 94.4 %cosine_convert_fusion.4 = bf16[768,8192]{1,0:T(8,128)(2,1)} fusion(s32[768]{0:T(1024)S(1)} %iota_add_fusion), kind=kLoop, calls=%fused_computation.7.clone.clone.1 | loop fusion | flops 94371840 | bytes 12585984 | tf_op jit(solution)/shard_map/dot_general | solution.py:19
  201.8 0.0 all-gather.2.cloned.1.call-done
  201.9 0.0 copy-start.1
  201.9 0.0 copy-start.4
  201.9 12.8 %fusion.14 = f32[768,512]{0,1:T(8,128)S(1)} fusion(bf16[8192,512]{0,1:T(8,128)(2,1)} %all-gather.2.cloned.1.call-done, bf16[768,8192]{1,0:T(8,128)(2,1)} %sine_convert_fusion.6), kind=kOutput, calls=%fused_computation.20 | convolution fusion | flops 6442844160 | bytes 22544384 | tf_op jit(solution)/shard_map/dot_general | solution.py:20
  214.7 0.0 copy-done.1
  214.7 0.2 copy-done.4
  214.9 6.7 %fusion.6 = f32[768,512]{0,1:T(8,128)S(1)} fusion(bf16[8192,512]{0,1:T(8,128)(2,1)S(1)} %copy-done.4, bf16[768,8192]{1,0:T(8,128)(2,1)S(1)} %copy-done.1), kind=kOutput, calls=%fused_computation.11 | convolution fusion | flops 6442450944 | bytes 22544384 | tf_op jit(solution)/shard_map/dot_general | solution.py:19
  221.7 1.9 pad_maximum_fusion
  223.6 6.8 %copy.15 = f32[768,2,8,64]{3,2,1,0:T(8,128)} copy(f32[768,2,8,64]{0,3,2,1:T(8,128)} %bitcast.34) | data formatting | bytes 6291456 | tf_op jit(solution)/shard_map/reshape | solution.py:45
  230.4 0.0 copy-start.3
  230.4 0.0 copy-start.2
  230.4 8.6 %fusion.13 = bf16[4,768,2,64]{3,0,2,1:T(4,128)(2,1)} fusion(f32[768,2,8,64]{3,2,1,0:T(8,128)} %copy.15, f32[8,768,4,1]{0,2,3,1:T(4,128)S(1)} %copy.19), kind=kOutput, calls=%fused_computation.19 | convolution fusion | flops 38141952 | bytes 4030464 | tf_op jit(solution)/shard_map/rmk,mtrc->kmtc/dot_general | solution.py:47
  239.0 3.5 copy.17
  242.5 0.0 reduce-scatter.3.cloned.1.call-update
  242.5 0.0 reduce-scatter.5.cloned.1.call-start
  242.6 0.0 copy-done.3
  242.6 26.1 %reduce-scatter.3.cloned.1.call-done = bf16[1,768,2,64]{1,3,2,0:T(8,128)(2,1)} async-done(((bf16[4,768,2,64]{1,3,2,0:T(8,128)(2,1)}), bf16[1,768,2,64]{1,3,2,0:T(8,128)(2,1)}) %reduce-scatter.3.cloned.1.call-update) | async-done | bytes 196624 | tf_op jit(solution)/shard_map/reduce_scatter | solution.py:46
  268.7 0.0 copy-done.2
  268.7 1.2 fusion.15
  269.9 0.0 copy-done
  269.9 1.4 fusion.16
  271.4 0.0 reduce-scatter.5.cloned.1.call-update
  271.4 132.8 %reduce-scatter.5.cloned.1.call-done = f32[64,16]{0,1:T(8,128)} async-done(((f32[64,512]{0,1:T(8,128)}), f32[64,16]{0,1:T(8,128)}) %reduce-scatter.5.cloned.1.call-update) | async-done | bytes 4112 | tf_op jit(solution)/shard_map/reduce_scatter | solution.py:59
  (2 shorter events, 0.0 us)
Async XLA Ops:
  6.5 263.4 %copy-start = (bf16[1,768,2,512]{3,2,1,0:T(2,128)(2,1)S(1)}, bf16[1,768,2,512]{3,2,1,0:T(2,128)(2,1)}, u32[]{:S(2)}) copy-start(bf16[1,768,2,512]{3,2,1,0:T(2,128)(2,1)} %param.13) | copy-start | bytes 4718596
  6.5 195.3 %all-gather.2.cloned.1.call-start = ((), (), s32[]{:S(2)}) async-start(), calls=%async_computation.2 | async-start | bytes 9437184 | tf_op jit(solution)/shard_map/all_gather | solution.py:42
  10.7 258.0 %reduce-scatter.3.cloned.1.call-start = ((), (), s32[]{:S(2)}) async-start(), calls=%async_computation.3 | async-start | bytes 983040 | tf_op jit(solution)/shard_map/reduce_scatter | solution.py:46
  201.9 12.9 %copy-start.1 = (bf16[768,8192]{1,0:T(8,128)(2,1)S(1)}, bf16[768,8192]{1,0:T(8,128)(2,1)}, u32[]{:S(2)}) copy-start(bf16[768,8192]{1,0:T(8,128)(2,1)} %cosine_convert_fusion.4) | copy-start | bytes 37748740
  201.9 13.1 %copy-start.4 = (bf16[8192,512]{0,1:T(8,128)(2,1)S(1)}, bf16[8192,512]{0,1:T(8,128)(2,1)}, u32[]{:S(2)}) copy-start(bf16[8192,512]{0,1:T(8,128)(2,1)} %all-gather.2.cloned.1.call-done) | copy-start | bytes 25165828
  230.4 12.2 %copy-start.3 = (f32[768,1]{0,1:T(1,128)S(1)}, f32[768,1]{0,1:T(1,128)}, u32[]{:S(2)}) copy-start(f32[768,1]{0,1:T(1,128)} %param.11) | copy-start | bytes 9220
  230.4 38.3 %copy-start.2 = (f32[64,64]{1,0:T(8,128)S(1)}, f32[64,64]{1,0:T(8,128)}, u32[]{:S(2)}) copy-start(f32[64,64]{1,0:T(8,128)} %param.12) | copy-start | bytes 49156
  242.5 161.7 %reduce-scatter.5.cloned.1.call-start = ((), (), s32[]{:S(2)}) async-start(), calls=%async_computation.4 | async-start | bytes 270336 | tf_op jit(solution)/shard_map/reduce_scatter | solution.py:59
Sparse Core Ops, SparseCore 0:
  10.8 57.2 all-gather.1
  242.7 25.9 reduce-scatter.2
  271.5 132.6 reduce-scatter.4
where the time goes:
time: 411 us
  other arithmetic  192 us (47%)
  waiting for transfers between devices  159 us (39%)
  matrix products  34.1 us (8%)
  between operations  13.2 us (3%)
  local copies, waits for them, and re-layouts  12 us (3%)
    reduce_scatter x1, waiting for transfers between devices, local(): lax.psum_scatter(partial_sketch, ('patch', 'mode'), scatter_dimension=1,...  133 us
    dot_general x1, other arithmetic, fourier(): imag_part = -jnp.dot(sine, values, preferred_element_type=jnp.float32)  95.2 us
    dot_general x1, other arithmetic, fourier(): real_part = jnp.dot(cosine, values, preferred_element_type=jnp.float32)  94.4 us
    reduce_scatter x1, waiting for transfers between devices, local(): lax.psum_scatter(jnp.einsum('rmk,mtrc->kmtc', cycle_legendre, four, preci...  26.1 us
    dot_general x1, matrix products, fourier(): imag_part = -jnp.dot(sine, values, preferred_element_type=jnp.float32)  12.8 us
    dot_general x1, matrix products, local(): jnp.einsum('rmk,mtrc->kmtc', cycle_legendre, four, precision=lax.Precisio...  8.64 us
  transfers between devices with their start and end apart: 3, of which 2 were waited for; matrix products, arithmetic and copies ran while one was open for 47% of the time, Pallas kernels for 0%

commit v1 on v0

v1 whole, which is shorter than its diff:
```python
import math

import jax
import jax.numpy as jnp
import ml_dtypes
import numpy as np
from jax import lax
from jax.experimental import pallas as pl
from jax.experimental.pallas import tpu as pltpu
from jax.sharding import PartitionSpec as P

LANES = 128
MIB = 1 << 20


def rotate(value, step, points):
    re, im = value
    step %= points
    if step == 0:
        return re, im
    if 2 * step == points:
        return -re, -im
    if 4 * step == points:
        return im, -re
    if 8 * step == points:
        return (re + im) * math.sqrt(0.5), (im - re) * math.sqrt(0.5)
    if 8 * step == 3 * points:
        return (im - re) * math.sqrt(0.5), (re + im) * -math.sqrt(0.5)
    c, s = math.cos(2 * math.pi * step / points), math.sin(2 * math.pi * step / points)
    return re * c + im * s, im * c - re * s


def dft(values):
    n = len(values)
    if n == 1:
        return values
    half = n // 2
    even, odd = dft(values[0::2]), dft(values[1::2])
    out = [None] * n
    for b in range(half):
        re, im = rotate(odd[b], b, n)
        out[b] = even[b][0] + re, even[b][1] + im
        out[b + half] = even[b][0] - re, even[b][1] - im
    return out


def whiten_kernel(sky_hbm, mask_hbm, factor_hbm, leg_hbm, sort_hbm, out_ref, sky, mask, factor, leg, sort, white, sems):
    cycles, chans, pixels = sky.shape
    groups = out_ref.shape[0]
    width = chans // groups
    split = pixels // LANES
    sources, targets = (sky_hbm, mask_hbm, factor_hbm, leg_hbm, sort_hbm), (sky, mask, factor, leg, sort)
    copies = [pltpu.make_async_copy(a, b, sems.at[n]) for n, (a, b) in enumerate(zip(sources, targets))]
    for copy in copies:
        copy.start()
    for copy in copies[:3]:
        copy.wait()
    for r in range(cycles):
        high = factor[r].astype(jnp.bfloat16)
        low = (factor[r] - high.astype(jnp.float32)).astype(jnp.bfloat16)
        both = jnp.concatenate([high, low], axis=1)
        pair = jnp.concatenate([sky[r], sky[r]], axis=0)
        value = jnp.dot(both, pair, preferred_element_type=jnp.float32)
        value = value * mask[r : r + 1, :].astype(jnp.float32)
        white[r * chans : (r + 1) * chans, :] = value.astype(jnp.bfloat16)
    copies[3].wait()
    rows = jnp.concatenate([leg[r] for r in range(cycles)], axis=0).astype(jnp.bfloat16)
    count = rows.shape[0]
    start = split * cycles * width
    for n in range(rows.shape[1] // LANES):
        for e in range(groups):
            out_ref[e, start + n * count : start + (n + 1) * count, :] = rows[:, n * LANES : (n + 1) * LANES]
    copies[4].wait()
    for pair in range(split // 2):
        wide = slice(pair * 2 * LANES, (pair + 1) * 2 * LANES)
        value = jnp.dot(white[...], sort[:, wide], preferred_element_type=jnp.float32)
        for half in range(2):
            s = pair * 2 + half
            part = value[:, half * LANES : (half + 1) * LANES]
            part = part.reshape(cycles, groups, width, LANES)
            part = jnp.swapaxes(part, 0, 1).reshape(groups, cycles * width, LANES).astype(jnp.bfloat16)
            out_ref[:, s * cycles * width : (s + 1) * cycles * width, :] = part


def modes_kernel(cycles, offsets, z_ref, twiddle_ref, table_hbm, out_ref, table, left, leg, prod_a, prod_b, x_ref, sems):
    sources = z_ref.shape[0]
    tiles = table.shape[0]
    split = twiddle_ref.shape[1]
    rows = left.shape[0]
    width = rows // (cycles * split)
    blocks = leg.shape[1] // (tiles * LANES)
    per = out_ref.shape[3] // LANES
    copies = [pltpu.make_async_copy(table_hbm.at[n], table.at[n], sems.at[n]) for n in range(tiles)]
    for copy in copies:
        copy.start()
    count = cycles * offsets
    for q in range(sources):
        left[:, q * LANES : (q + 1) * LANES] = z_ref[q, :rows, :]
        for n in range(per):
            place = (q * per + n) * LANES
            leg[:, place : place + LANES] = z_ref[q, rows + n * count : rows + (n + 1) * count, :].astype(jnp.float32)

    def product(tile, prod):
        copies[tile].wait()
        prod[...] = jnp.dot(left[...], table[tile], preferred_element_type=jnp.float32)

    def use(tile, prod):
        lanes = slice(tile * LANES, (tile + 1) * LANES)
        cosine, sine = twiddle_ref[0, :, lanes], twiddle_ref[1, :, lanes]
        for r in range(cycles):
            values = []
            for s in range(split):
                place = (s * cycles + r) * width
                re = prod[place : place + width, :LANES]
                im = prod[place : place + width, LANES:]
                if s == 0:
                    values.append((re, -im))
                else:
                    c, d = cosine[s : s + 1, :], sine[s : s + 1, :]
                    values.append((re * c - im * d, -(re * d) - im * c))
            parts = dft(values)
            for b in range(blocks):
                x_ref[b, 0, r] = parts[b][0]
                x_ref[b, 1, r] = parts[b][1]
        for b in range(blocks):
            mode_tile = b * tiles + tile
            d, n = mode_tile // per, mode_tile % per
            mode = slice(mode_tile * LANES, (mode_tile + 1) * LANES)
            for k in range(offsets):
                total = [None, None]
                for r in range(cycles):
                    row = leg[r * offsets + k : r * offsets + k + 1, mode]
                    for t in range(2):
                        term = row * x_ref[b, t, r]
                        total[t] = term if r == 0 else total[t] + term
                out_ref[k, d, :, n * LANES : (n + 1) * LANES] = jnp.concatenate(total, axis=0).astype(jnp.bfloat16)

    prods = (prod_a, prod_b)
    product(0, prods[0])
    for tile in range(tiles):
        if tile + 1 < tiles:
            product(tile + 1, prods[(tile + 1) % 2])
        use(tile, prods[tile % 2])


def sketch_kernel(alm_ref, band_ref, cov_ref, test_ref, out_ref, left_ref):
    patches, groups, rows, lanes = alm_ref.shape
    chans = cov_ref.shape[0]
    width = rows // 2
    for g in range(groups):
        part = alm_ref[0, g].astype(jnp.float32)
        for p in range(1, patches):
            part += alm_ref[p, g].astype(jnp.float32)
        part = part * band_ref[...]
        for t in range(2):
            left_ref[t, g * width : (g + 1) * width, :] = part[t * width : (t + 1) * width]
    sketch = None
    for t in range(2):
        term = lax.dot_general(
            test_ref[t],
            left_ref[t].astype(jnp.bfloat16),
            (((0,), (1,)), ((), ())),
            preferred_element_type=jnp.float32,
        )
        sketch = term if t == 0 else sketch + term
    mixed = lax.dot_general(
        sketch,
        cov_ref[...],
        (((1,), (1,)), ((), ())),
        precision=lax.Precision.HIGHEST,
        preferred_element_type=jnp.float32,
    )
    if out_ref.ndim == 2:
        out_ref[...] = mixed
    else:
        owners, block, _ = out_ref.shape
        fold = out_ref.shape[2] // chans
        mixed = mixed.reshape(owners, fold, block, chans)
        out_ref[...] = jnp.concatenate([mixed[:, n] for n in range(fold)], axis=-1)


def total_kernel(part_ref, out_ref):
    block, chans = part_ref.shape[1], out_ref.shape[1]
    total = jnp.sum(part_ref[...], axis=0)
    for n in range(part_ref.shape[2] // chans):
        out_ref[n * block : (n + 1) * block, :] = total[:, n * chans : (n + 1) * chans]


def call(kernel, shape, dtype, scratch, mib, spaces, *operands):
    return pl.pallas_call(
        kernel,
        out_shape=jax.ShapeDtypeStruct(shape, dtype),
        in_specs=[pl.BlockSpec(memory_space=space) for space in spaces],
        out_specs=pl.BlockSpec(memory_space=pltpu.VMEM),
        scratch_shapes=scratch,
        compiler_params=pltpu.CompilerParams(vmem_limit_bytes=mib * MIB),
    )(*operands)


def transform_tables(split, cycle):
    half = cycle // split
    step = np.arange(split)[:, None] * np.arange(half)[None, :] % cycle
    angle = step * (2.0 * math.pi / cycle)
    twiddle = np.stack([np.cos(angle), np.sin(angle)]).astype(np.float32)
    step = np.arange(half)[:, None] * np.arange(half)[None, :] % half
    angle = (step * (2.0 * math.pi / half)).reshape(half, half // LANES, LANES)
    table = np.transpose(np.concatenate([np.cos(angle), np.sin(angle)], axis=2), (1, 0, 2))
    return twiddle, table.astype(ml_dtypes.bfloat16)


def sorting(pixels, split):
    place = np.arange(pixels) % split * (pixels // split) + np.arange(pixels) // split
    return (place[:, None] == np.arange(pixels)[None, :]).astype(ml_dtypes.bfloat16)


def local(sky_map, pixel_mask, noise_factor, cycle_legendre, band_power, channel_cov, test_matrix):
    cycles, pixels, chans = sky_map.shape
    modes, _ = band_power.shape
    offsets = cycle_legendre.shape[2]
    columns = test_matrix.shape[3]
    mode_count, patches = lax.axis_size("mode"), lax.axis_size("patch")
    width = chans // mode_count
    split = pixels // LANES
    rows = split * cycles * width
    legs = cycles * offsets * (modes // LANES)
    tiles = mode_count
    everyone = ("patch", "mode")
    hbm, vmem, bf16, f32 = pl.ANY, pltpu.VMEM, jnp.bfloat16, jnp.float32

    message = call(
        whiten_kernel,
        (mode_count, rows + legs, LANES),
        bf16,
        [
            vmem((cycles, chans, pixels), bf16),
            vmem((cycles, pixels), jnp.int32),
            vmem((cycles, chans, chans), f32),
            vmem((cycles, offsets, modes), f32),
            vmem((pixels, pixels), bf16),
            vmem((cycles * chans, pixels), bf16),
            pltpu.SemaphoreType.DMA((5,)),
        ],
        56,
        [hbm] * 5,
        jnp.transpose(sky_map, (0, 2, 1)),
        pixel_mask,
        noise_factor[:, 0],
        jnp.transpose(cycle_legendre, (0, 2, 1)),
        jnp.asarray(sorting(pixels, split)),
    )
    message = lax.all_to_all(message, "mode", 0, 0, tiled=True)

    twiddle, table = transform_tables(split, pixels * mode_count)
    blocks = modes * mode_count // (tiles * LANES)
    alm = call(
        lambda *refs: modes_kernel(cycles, offsets, *refs),
        (offsets, mode_count, 2 * width, modes),
        bf16,
        [
            vmem((tiles, tiles * LANES, 2 * LANES), bf16),
            vmem((rows, tiles * LANES), bf16),
            vmem((cycles * offsets, mode_count * modes), f32),
            vmem((rows, 2 * LANES), f32),
            vmem((rows, 2 * LANES), f32),
            vmem((blocks, 2, cycles, width, LANES), f32),
            pltpu.SemaphoreType.DMA((tiles,)),
        ],
        56,
        [vmem, vmem, hbm],
        message,
        jnp.asarray(twiddle),
        jnp.asarray(table),
    )
    alm = alm.reshape(patches * mode_count, 2 * width, modes)
    alm = lax.all_to_all(alm, everyone, 0, 0, tiled=True)
    alm = alm.reshape(patches, mode_count, 2 * width, modes)

    share = columns // (patches * mode_count)
    fold = LANES // chans
    packed = share % (8 * fold) == 0
    part = call(
        sketch_kernel,
        (patches * mode_count, share // fold, LANES) if packed else (columns, chans),
        f32,
        [vmem((2, chans, modes), f32)],
        24,
        [vmem] * 4,
        alm,
        jnp.transpose(band_power),
        channel_cov,
        jnp.transpose(test_matrix[0], (1, 0, 2)),
    )
    if not packed:
        part = part.reshape(patches * mode_count, share, chans)
    part = lax.all_to_all(part, everyone, 0, 0, tiled=True)
    return jnp.transpose(call(total_kernel, (share, chans), f32, [], 16, [vmem], part))


def solution(mesh):
    return jax.shard_map(
        local,
        mesh=mesh,
        in_specs=(
            P("patch", "mode", None),
            P("patch", "mode"),
            P("patch", "mode", None, None),
            P("patch", "mode", None),
            P("mode", "patch"),
            P(),
            P("patch", "mode", None, None),
        ),
        out_specs=P(None, ("patch", "mode")),
        check_vma=False,
    )
```

time: 411 us -> 78.7 us (0.19)
  other arithmetic: 192 us -> 0 us
  waiting for transfers between devices: 159 us -> 18.9 us
  blocking collectives: 0 us -> 36.5 us
  matrix products: 34.1 us -> 0 us
  Pallas kernels: 0 us -> 16.8 us
  between operations: 13.2 us -> 0.05 us
  local copies, waits for them, and re-layouts: 12 us -> 1.68 us
  starting transfers between devices: 0.09 us -> 4.41 us
    dot_general x2 -> x0, other arithmetic: 190 us -> none  [the longest x1 95.2 us: fourier(): imag_part = -jnp.dot(sine, values, preferred_element_type=jnp.float32)]
    reduce_scatter x2 -> x0, waiting for transfers between devices: 159 us -> none  [the longest x1 133 us: local(): lax.psum_scatter(partial_sketch, ('patch', 'mode'), scatter_dimension=1,...]
    all_to_all x0 -> x2, blocking collectives: none -> 36.5 us  [the longest x1 24.9 us: local(): message = lax.all_to_all(message, 'mode', 0, 0, tiled=True)]
    dot_general x6 -> x0, matrix products: 34.1 us -> none  [the longest x1 12.8 us: fourier(): imag_part = -jnp.dot(sine, values, preferred_element_type=jnp.float32)]
    all_to_all x0 -> x1, waiting for transfers between devices: none -> 18.9 us  [local(): alm = lax.all_to_all(alm, everyone, 0, 0, tiled=True)]
    pallas_call x0 -> x4, Pallas kernels: none -> 16.8 us  [call(): pl.pallas_call(kernel, out_shape=jax.ShapeDtypeStruct(shape, dtype), in_s...]
    reshape x1 -> x0, local copies, waits for them, and re-layouts: 6.83 us -> none  [local(): four = four.reshape(mode_count, 2, cycle_count, chans)]
    all_to_all x0 -> x1, starting transfers between devices: none -> 4.41 us  [local(): alm = lax.all_to_all(alm, everyone, 0, 0, tiled=True)]
  transfers between devices with their start and end apart: 3 -> 1, of which waited for: 2 -> 1; matrix products, arithmetic and copies ran while one was open for 47% -> 2% of each run, Pallas kernels for 0% -> 0%
where the time goes in v1:
time: 78.7 us; the launch traced here: 78.4 us
  blocking collectives  36.5 us (46%)
  waiting for transfers between devices  18.9 us (24%)
  Pallas kernels  16.8 us (21%)
  starting transfers between devices  4.41 us (6%)
  local copies, waits for them, and re-layouts  1.68 us (2%)
    all_to_all x1, blocking collectives, local(): message = lax.all_to_all(message, 'mode', 0, 0, tiled=True)  24.9 us
    all_to_all x1, waiting for transfers between devices, local(): alm = lax.all_to_all(alm, everyone, 0, 0, tiled=True)  18.9 us
    pallas_call x4, Pallas kernels, call(): pl.pallas_call(kernel, out_shape=jax.ShapeDtypeStruct(shape, dtype), in_s...  16.8 us
    all_to_all x1, blocking collectives, local(): part = lax.all_to_all(part, everyone, 0, 0, tiled=True)  11.7 us
    all_to_all x1, starting transfers between devices, local(): alm = lax.all_to_all(alm, everyone, 0, 0, tiled=True)  4.41 us
    unnamed x5, local copies, waits for them, and re-layouts  1.68 us
  transfers between devices with their start and end apart: 1, of which 1 were waited for; matrix products, arithmetic and copies ran while one was open for 2% of the time, Pallas kernels for 0%

profile of v1, /device:TPU:0, one launch (start us, length us, event | category | flops | bytes accessed | tf_op | source)
XLA Modules:
  0.0 78.4 jit_solution(16955006543292841767)
XLA Ops:
  0.0 4.5 %shard_map.100 = bf16[8,704,128]{2,1,0:T(8,128)(2,1)} custom-call(bf16[8,64,1024]{2,1,0:T(8,128)(2,1)} %bitcast.16, s32[8,1024]{1,0:T(8,128)} %mask_hbm.1, f32[8,64,64]{2,1,0:T(8,128)} %bitcast.17, f32[8,4,768]{2,1,0:T(4,128)} %bitcast.18, bf16[1024,1024]{1,0:T(8,128)(2,1)} %constant.6.clone.sort_hbm), custom_call_target="tpu_custom_call" | custom-call | tf_op jit(solution)/shard_map/pallas_call | solution.py:190
  4.5 24.9 %all_to_all.15.refs_0_ = bf16[8,704,128]{2,1,0:T(8,128)(2,1)} all-to-all(bf16[8,704,128]{2,1,0:T(8,128)(2,1)} %shard_map.100), channel_id=1, replica_groups=mesh['patch'=4,'mode'=8] {'mode'}, dimensions={0} | all-to-all | bytes 2883584 | tf_op jit(solution)/shard_map/all_to_all | solution.py:251
  29.3 10.3 %shard_map.101 = bf16[4,8,16,768]{3,2,1,0:T(8,128)(2,1)} custom-call(bf16[8,704,128]{2,1,0:T(8,128)(2,1)} %all_to_all.15.refs_0_, f32[2,8,1024]{2,1,0:T(8,128)} %constant.7.clone.refs_1_, bf16[8,1024,256]{2,1,0:T(8,128)(2,1)} %constant.8.clone.refs_2_), custom_call_target="tpu_custom_call" | custom-call | tf_op jit(solution)/shard_map/pallas_call | solution.py:190
  39.7 4.4 %all-to-all-start.1 = ((bf16[32,16,768]{2,1,0:T(8,128)(2,1)}), bf16[32,16,768]{2,1,0:T(8,128)(2,1)S(1)}, u32[]{:S(2)}, u32[]{:S(2)}) async-start(bf16[32,16,768]{2,1,0:T(8,128)(2,1)} %bitcast.15), calls=%async_computation.1 | async-start | bytes 1572864 | tf_op jit(solution)/shard_map/all_to_all | solution.py:275
  44.1 0.0 copy-start
  44.1 0.0 copy-start.1
  44.1 1.7 %copy.13 = bf16[1,768,2,512]{3,1,2,0:T(8,128)(2,1)S(1)} copy(bf16[1,768,2,512]{3,2,1,0:T(2,128)(2,1)} %param.16) | data formatting | bytes 3145728 | tf_op args[6]
  45.8 18.9 %all-to-all-done.1 = bf16[32,16,768]{2,1,0:T(8,128)(2,1)S(1)} async-done(((bf16[32,16,768]{2,1,0:T(8,128)(2,1)}), bf16[32,16,768]{2,1,0:T(8,128)(2,1)S(1)}, u32[]{:S(2)}, u32[]{:S(2)}) %all-to-all-start.1) | async-done | bytes 786464 | tf_op jit(solution)/shard_map/all_to_all | solution.py:275
  64.7 0.0 copy-done
  64.7 0.0 copy-done.1
  64.7 1.3 %shard_map.102 = f32[32,8,128]{2,1,0:T(8,128)S(1)} custom-call(bf16[4,8,16,768]{3,2,1,0:T(8,128)(2,1)S(1)} %bitcast.13, f32[1,768]{1,0:T(1,128)S(1)} %bitcast.14, f32[64,64]{1,0:T(8,128)S(1)} %copy-done, bf16[2,768,512]{2,1,0:T(8,128)(2,1)S(1)} %bitcast.12), custom_call_target="tpu_custom_call" | custom-call | tf_op jit(solution)/shard_map/pallas_call | solution.py:190
  66.0 11.7 %all_to_all.16.part_ref = f32[32,8,128]{2,1,0:T(8,128)S(1)} all-to-all(f32[32,8,128]{2,1,0:T(8,128)S(1)} %shard_map.102), channel_id=1, replica_groups=mesh['patch'=4,'mode'=8] {'patch','mode'}, dimensions={0} | all-to-all | bytes 262144 | tf_op jit(solution)/shard_map/all_to_all | solution.py:295
  77.7 0.7 shard_map.103
Async XLA Ops:
  39.7 25.0 %all-to-all-start.1 = ((bf16[32,16,768]{2,1,0:T(8,128)(2,1)}), bf16[32,16,768]{2,1,0:T(8,128)(2,1)S(1)}, u32[]{:S(2)}, u32[]{:S(2)}) async-start(bf16[32,16,768]{2,1,0:T(8,128)(2,1)} %bitcast.15), calls=%async_computation.1 | async-start | bytes 1572864 | tf_op jit(solution)/shard_map/all_to_all | solution.py:275
  44.1 20.6 %copy-start = (f32[64,64]{1,0:T(8,128)S(1)}, f32[64,64]{1,0:T(8,128)}, u32[]{:S(2)}) copy-start(f32[64,64]{1,0:T(8,128)} %cov_ref.1) | copy-start | bytes 49156
  44.1 20.6 %copy-start.1 = (f32[768,1]{0,1:T(1,128)S(1)}, f32[768,1]{0,1:T(1,128)}, u32[]{:S(2)}) copy-start(f32[768,1]{0,1:T(1,128)} %param.14) | copy-start | bytes 9220

commit v2 on v1

--- a/solution.py
+++ b/solution.py
@@ -44,9 +44,11 @@
     return out
 
 
-def whiten_kernel(sky_hbm, mask_hbm, factor_hbm, leg_hbm, sort_hbm, out_ref, sky, mask, factor, leg, sort, white, sems):
+def whiten_kernel(me_ref, sky_hbm, mask_hbm, factor_hbm, leg_hbm, sort_hbm, *refs):
+    sky, mask, factor, leg, sort, white, stage, sems = refs[-8:]
+    outs = refs[:-8]
     cycles, chans, pixels = sky.shape
-    groups = out_ref.shape[0]
+    groups = len(outs)
     width = chans // groups
     split = pixels // LANES
     sources, targets = (sky_hbm, mask_hbm, factor_hbm, leg_hbm, sort_hbm), (sky, mask, factor, leg, sort)
@@ -69,7 +71,7 @@
     start = split * cycles * width
     for n in range(rows.shape[1] // LANES):
         for e in range(groups):
-            out_ref[e, start + n * count : start + (n + 1) * count, :] = rows[:, n * LANES : (n + 1) * LANES]
+            stage[e, start + n * count : start + (n + 1) * count, :] = rows[:, n * LANES : (n + 1) * LANES]
     copies[4].wait()
     for pair in range(split // 2):
         wide = slice(pair * 2 * LANES, (pair + 1) * 2 * LANES)
@@ -79,33 +81,45 @@
             part = value[:, half * LANES : (half + 1) * LANES]
             part = part.reshape(cycles, groups, width, LANES)
             part = jnp.swapaxes(part, 0, 1).reshape(groups, cycles * width, LANES).astype(jnp.bfloat16)
-            out_ref[:, s * cycles * width : (s + 1) * cycles * width, :] = part
-
-
-def modes_kernel(cycles, offsets, z_ref, twiddle_ref, table_hbm, out_ref, table, left, leg, prod_a, prod_b, x_ref, sems):
-    sources = z_ref.shape[0]
+            stage[:, s * cycles * width : (s + 1) * cycles * width, :] = part
+    me = me_ref[0]
+    sends = [
+        pltpu.make_async_copy(stage.at[jnp.bitwise_xor(me, n)], outs[n], sems.at[5 + n]) for n in range(groups)
+    ]
+    for send in sends:
+        send.start()
+    for send in sends:
+        send.wait()
+
+
+def modes_kernel(cycles, offsets, sources, me_ref, twiddle_ref, table_hbm, *refs):
+    slots = refs[:sources]
+    out_ref, table, left, leg, prod_a, prod_b, x_ref, table_sems = refs[sources:]
     tiles = table.shape[0]
     split = twiddle_ref.shape[1]
     rows = left.shape[0]
     width = rows // (cycles * split)
     blocks = leg.shape[1] // (tiles * LANES)
     per = out_ref.shape[3] // LANES
-    copies = [pltpu.make_async_copy(table_hbm.at[n], table.at[n], sems.at[n]) for n in range(tiles)]
-    for copy in copies:
-        copy.start()
     count = cycles * offsets
-    for q in range(sources):
-        left[:, q * LANES : (q + 1) * LANES] = z_ref[q, :rows, :]
+    me = me_ref[0]
+    def copy(tile):
+        return pltpu.make_async_copy(table_hbm.at[tile], table.at[tile], table_sems.at[tile])
+
+    for tile in range(tiles):
+        copy(tile).start()
+    for slot in range(sources):
+        q = jnp.bitwise_xor(me, slot)
+        left[:, pl.ds(pl.multiple_of(q * LANES, LANES), LANES)] = slots[slot][:rows, :]
         for n in range(per):
-            place = (q * per + n) * LANES
-            leg[:, place : place + LANES] = z_ref[q, rows + n * count : rows + (n + 1) * count, :].astype(jnp.float32)
+            lanes = pl.ds(pl.multiple_of((q * per + n) * LANES, LANES), LANES)
+            leg[:, lanes] = slots[slot][rows + n * count : rows + (n + 1) * count, :].astype(jnp.float32)
 
     def product(tile, prod):
-        copies[tile].wait()
         prod[...] = jnp.dot(left[...], table[tile], preferred_element_type=jnp.float32)
 
     def use(tile, prod):
-        lanes = slice(tile * LANES, (tile + 1) * LANES)
+        lanes = pl.ds(pl.multiple_of(tile * LANES, LANES), LANES)
         cosine, sine = twiddle_ref[0, :, lanes], twiddle_ref[1, :, lanes]
         for r in range(cycles):
             values = []
@@ -125,7 +139,7 @@
         for b in range(blocks):
             mode_tile = b * tiles + tile
             d, n = mode_tile // per, mode_tile % per
-            mode = slice(mode_tile * LANES, (mode_tile + 1) * LANES)
+            mode = pl.ds(pl.multiple_of(mode_tile * LANES, LANES), LANES)
             for k in range(offsets):
                 total = [None, None]
                 for r in range(cycles):
@@ -133,14 +147,24 @@
                     for t in range(2):
                         term = row * x_ref[b, t, r]
                         total[t] = term if r == 0 else total[t] + term
-                out_ref[k, d, :, n * LANES : (n + 1) * LANES] = jnp.concatenate(total, axis=0).astype(jnp.bfloat16)
-
-    prods = (prod_a, prod_b)
-    product(0, prods[0])
-    for tile in range(tiles):
-        if tile + 1 < tiles:
-            product(tile + 1, prods[(tile + 1) % 2])
-        use(tile, prods[tile % 2])
+                place = pl.ds(pl.multiple_of(n * LANES, LANES), LANES)
+                out_ref[k, d, :, place] = jnp.concatenate(total, axis=0).astype(jnp.bfloat16)
+
+    copy(0).wait()
+    product(0, prod_a)
+
+    @pl.loop(0, tiles // 2)
+    def _(step):
+        copy(2 * step + 1).wait()
+
+        @pl.when(2 * step + 2 < tiles)
+        def _():
+            copy(2 * step + 2).wait()
+
+        product(2 * step + 1, prod_b)
+        use(2 * step, prod_a)
+        product(jnp.minimum(2 * step + 2, tiles - 1), prod_a)
+        use(2 * step + 1, prod_b)
 
 
 def sketch_kernel(alm_ref, band_ref, cov_ref, test_ref, out_ref, left_ref):
@@ -186,12 +210,12 @@
         out_ref[n * block : (n + 1) * block, :] = total[:, n * chans : (n + 1) * chans]
 
 
-def call(kernel, shape, dtype, scratch, mib, spaces, *operands):
+def call(kernel, shape, scratch, mib, spaces, *operands, out_space=pltpu.VMEM):
     return pl.pallas_call(
         kernel,
-        out_shape=jax.ShapeDtypeStruct(shape, dtype),
+        out_shape=shape,
         in_specs=[pl.BlockSpec(memory_space=space) for space in spaces],
-        out_specs=pl.BlockSpec(memory_space=pltpu.VMEM),
+        out_specs=jax.tree.map(lambda _: pl.BlockSpec(memory_space=out_space), shape),
         scratch_shapes=scratch,
         compiler_params=pltpu.CompilerParams(vmem_limit_bytes=mib * MIB),
     )(*operands)
@@ -227,10 +251,11 @@
     everyone = ("patch", "mode")
     hbm, vmem, bf16, f32 = pl.ANY, pltpu.VMEM, jnp.bfloat16, jnp.float32
 
-    message = call(
+    me = lax.axis_index("mode").astype(jnp.int32).reshape(1)
+    shape = jax.ShapeDtypeStruct
+    messages = call(
         whiten_kernel,
-        (mode_count, rows + legs, LANES),
-        bf16,
+        [shape((rows + legs, LANES), bf16)] * mode_count,
         [
             vmem((cycles, chans, pixels), bf16),
             vmem((cycles, pixels), jnp.int32),
@@ -238,24 +263,28 @@
             vmem((cycles, offsets, modes), f32),
             vmem((pixels, pixels), bf16),
             vmem((cycles * chans, pixels), bf16),
-            pltpu.SemaphoreType.DMA((5,)),
+            vmem((mode_count, rows + legs, LANES), bf16),
+            pltpu.SemaphoreType.DMA((5 + mode_count,)),
         ],
         56,
-        [hbm] * 5,
+        [pltpu.SMEM] + [hbm] * 5,
+        me,
         jnp.transpose(sky_map, (0, 2, 1)),
         pixel_mask,
         noise_factor[:, 0],
         jnp.transpose(cycle_legendre, (0, 2, 1)),
         jnp.asarray(sorting(pixels, split)),
-    )
-    message = lax.all_to_all(message, "mode", 0, 0, tiled=True)
+        out_space=hbm,
+    )
+    slots = [messages[0]]
+    for n in range(1, mode_count):
+        slots.append(lax.ppermute(messages[n], "mode", [(i, i ^ n) for i in range(mode_count)]))
 
     twiddle, table = transform_tables(split, pixels * mode_count)
     blocks = modes * mode_count // (tiles * LANES)
     alm = call(
-        lambda *refs: modes_kernel(cycles, offsets, *refs),
-        (offsets, mode_count, 2 * width, modes),
-        bf16,
+        lambda *refs: modes_kernel(cycles, offsets, mode_count, *refs),
+        shape((offsets, mode_count, 2 * width, modes), bf16),
         [
             vmem((tiles, tiles * LANES, 2 * LANES), bf16),
             vmem((rows, tiles * LANES), bf16),
@@ -266,10 +295,11 @@
             pltpu.SemaphoreType.DMA((tiles,)),
         ],
         56,
-        [vmem, vmem, hbm],
-        message,
+        [pltpu.SMEM, vmem, hbm] + [vmem] * mode_count,
+        me,
         jnp.asarray(twiddle),
         jnp.asarray(table),
+        *slots,
     )
     alm = alm.reshape(patches * mode_count, 2 * width, modes)
     alm = lax.all_to_all(alm, everyone, 0, 0, tiled=True)
@@ -280,8 +310,7 @@
     packed = share % (8 * fold) == 0
     part = call(
         sketch_kernel,
-        (patches * mode_count, share // fold, LANES) if packed else (columns, chans),
-        f32,
+        shape((patches * mode_count, share // fold, LANES) if packed else (columns, chans), f32),
         [vmem((2, chans, modes), f32)],
         24,
         [vmem] * 4,
@@ -293,7 +322,7 @@
     if not packed:
         part = part.reshape(patches * mode_count, share, chans)
     part = lax.all_to_all(part, everyone, 0, 0, tiled=True)
-    return jnp.transpose(call(total_kernel, (share, chans), f32, [], 16, [vmem], part))
+    return jnp.transpose(call(total_kernel, shape((share, chans), f32), [], 16, [vmem], part))
 
 
 def solution(mesh):

time: 78.7 us -> 75.6 us (0.961)
  blocking collectives: 36.5 us -> 11.7 us
  waiting for transfers between devices: 18.9 us -> 30.8 us
  starting transfers between devices: 4.41 us -> 15.4 us
  Pallas kernels: 16.8 us -> 14.8 us
    all_to_all x1 -> x0, blocking collectives: 24.9 us -> none  [local(): message = lax.all_to_all(message, 'mode', 0, 0, tiled=True)]
    ppermute x0 -> x7, waiting for transfers between devices: none -> 11.9 us  [local(): lax.ppermute(messages[n], 'mode', [(i, i ^ n) for i in range(mode_count)])]
    ppermute x0 -> x7, starting transfers between devices: none -> 9.25 us  [local(): lax.ppermute(messages[n], 'mode', [(i, i ^ n) for i in range(mode_count)])]
    pallas_call x4, Pallas kernels: 16.8 us -> 14.8 us  [call(): pl.pallas_call(kernel, out_shape=shape, in_specs=[pl.BlockSpec(memory_spa...]
    all_to_all x1, starting transfers between devices: 4.41 us -> 6.17 us  [local(): alm = lax.all_to_all(alm, everyone, 0, 0, tiled=True)]
    unnamed x5 -> x19, local copies, waits for them, and re-layouts: 1.68 us -> 2.43 us
  transfers between devices with their start and end apart: 1 -> 8, of which waited for: 1 -> 4; matrix products, arithmetic and copies ran while one was open for 2% -> 2% of each run, Pallas kernels for 0% -> 0%
where the time goes in v2:
time: 75.6 us; the launch traced here: 75.3 us
  waiting for transfers between devices  30.8 us (41%)
  starting transfers between devices  15.4 us (20%)
  Pallas kernels  14.8 us (20%)
  blocking collectives  11.7 us (15%)
  local copies, waits for them, and re-layouts  2.43 us (3%)
    all_to_all x1, waiting for transfers between devices, local(): alm = lax.all_to_all(alm, everyone, 0, 0, tiled=True)  19 us
    pallas_call x4, Pallas kernels, call(): pl.pallas_call(kernel, out_shape=shape, in_specs=[pl.BlockSpec(memory_spa...  14.8 us
    ppermute x7, waiting for transfers between devices, local(): lax.ppermute(messages[n], 'mode', [(i, i ^ n) for i in range(mode_count)])  11.9 us
    all_to_all x1, blocking collectives, local(): part = lax.all_to_all(part, everyone, 0, 0, tiled=True)  11.7 us
    ppermute x7, starting transfers between devices, local(): lax.ppermute(messages[n], 'mode', [(i, i ^ n) for i in range(mode_count)])  9.25 us
    all_to_all x1, starting transfers between devices, local(): alm = lax.all_to_all(alm, everyone, 0, 0, tiled=True)  6.17 us
    unnamed x19, local copies, waits for them, and re-layouts  2.43 us
  transfers between devices with their start and end apart: 8, of which 4 were waited for; matrix products, arithmetic and copies ran while one was open for 2% of the time, Pallas kernels for 0%

profile of v2, /device:TPU:0, one launch (start us, length us, event | category | flops | bytes accessed | tf_op | source)
XLA Modules:
  0.0 75.3 jit_solution(1891309769500093219)
XLA Ops:
  0.0 4.6 %shard_map.100 = (bf16[704,128]{1,0:T(8,128)(2,1)}, bf16[704,128]{1,0:T(8,128)(2,1)}, bf16[704,128]{1,0:T(8,128)(2,1)}, bf16[704,128]{1,0:T(8,128)(2,1)}, bf16[7...) custom-call(s32[1]{0:T(128)} %bitcast.me_ref.refs_0_, ...), custom_call_target="tpu_custom_call" | custom-call | tf_op jit(solution)/shard_map/pallas_call | solution.py:214
  4.6 0.5 collective-permute-start
  5.1 2.6 %collective-permute-start.1 = (bf16[704,128]{1,0:T(8,128)(2,1)}, bf16[704,128]{1,0:T(8,128)(2,1)S(1)}, u32[]{:S(2)}, u32[]{:S(2)}) collective-permute-start(bf16[704,128]{1,0:T(8,128)(2,1)} %get-tuple-element.15), channel_id=1, source_target_pairs={{0,2},{1,3},{2,0},{3,1},{4,6},{5,7},{6,4},{7,5},{8,10},{9,11},{10,... | collective-permute-start | bytes 540680 | tf_op jit(solution)/shard_map/ppermute | solution.py:281
  7.6 0.1 collective-permute-start.2
  7.7 1.8 %collective-permute-start.3 = (bf16[704,128]{1,0:T(8,128)(2,1)}, bf16[704,128]{1,0:T(8,128)(2,1)S(1)}, u32[]{:S(2)}, u32[]{:S(2)}) collective-permute-start(bf16[704,128]{1,0:T(8,128)(2,1)} %get-tuple-element.17), channel_id=1, source_target_pairs={{0,4},{1,5},{2,6},{3,7},{4,0},{5,1},{6,2},{7,3},{8,12},{9,13},{10,... | collective-permute-start | bytes 540680 | tf_op jit(solution)/shard_map/ppermute | solution.py:281
  9.5 0.0 collective-permute-start.4
  9.5 0.0 collective-permute-done.refs_4_
  9.5 0.0 copy-start.2
  9.5 2.6 %collective-permute-start.5 = (bf16[704,128]{1,0:T(8,128)(2,1)}, bf16[704,128]{1,0:T(8,128)(2,1)S(1)}, u32[]{:S(2)}, u32[]{:S(2)}) collective-permute-start(bf16[704,128]{1,0:T(8,128)(2,1)} %get-tuple-element.19), channel_id=1, source_target_pairs={{0,6},{1,7},{2,4},{3,5},{4,2},{5,3},{6,0},{7,1},{8,14},{9,15},{10,... | collective-permute-start | bytes 540680 | tf_op jit(solution)/shard_map/ppermute | solution.py:281
  12.1 1.2 %collective-permute-done.1.refs_5_ = bf16[704,128]{1,0:T(8,128)(2,1)S(1)} collective-permute-done((bf16[704,128]{1,0:T(8,128)(2,1)}, bf16[704,128]{1,0:T(8,128)(2,1)S(1)}, u32[]{:S(2)}, u32[]{:S(2)}) %collective-permute-start.1) | collective-permute-done | bytes 180256 | tf_op jit(solution)/shard_map/ppermute | solution.py:281
  13.3 0.0 copy-start.3
  13.3 1.7 %collective-permute-start.6 = (bf16[704,128]{1,0:T(8,128)(2,1)}, bf16[704,128]{1,0:T(8,128)(2,1)S(1)}, u32[]{:S(2)}, u32[]{:S(2)}) collective-permute-start(bf16[704,128]{1,0:T(8,128)(2,1)} %get-tuple-element.20), channel_id=1, source_target_pairs={{0,7},{1,6},{2,5},{3,4},{4,3},{5,2},{6,1},{7,0},{8,15},{9,14},{10,... | collective-permute-start | bytes 540680 | tf_op jit(solution)/shard_map/ppermute | solution.py:281
  15.0 1.7 %collective-permute-done.2.refs_6_ = bf16[704,128]{1,0:T(8,128)(2,1)S(1)} collective-permute-done((bf16[704,128]{1,0:T(8,128)(2,1)}, bf16[704,128]{1,0:T(8,128)(2,1)S(1)}, u32[]{:S(2)}, u32[]{:S(2)}) %collective-permute-start.2) | collective-permute-done | bytes 180256 | tf_op jit(solution)/shard_map/ppermute | solution.py:281
  16.7 0.0 copy-start.4
  16.7 0.0 collective-permute-done.3.refs_7_
  16.7 0.0 copy-start.5
  16.7 9.0 %collective-permute-done.4.refs_8_ = bf16[704,128]{1,0:T(8,128)(2,1)S(1)} collective-permute-done((bf16[704,128]{1,0:T(8,128)(2,1)}, bf16[704,128]{1,0:T(8,128)(2,1)S(1)}, u32[]{:S(2)}, u32[]{:S(2)}) %collective-permute-start.4) | collective-permute-done | bytes 180256 | tf_op jit(solution)/shard_map/ppermute | solution.py:281
  25.7 0.0 copy-start.6
  25.7 0.0 collective-permute-done.5.refs_9_
  25.7 0.0 copy-start.7
  25.7 0.0 collective-permute-done.6.refs_10_
  25.7 0.0 copy-start.8
  25.7 0.0 copy-done.2
  25.7 0.0 copy-done.3
  25.7 0.0 copy-done.4
  25.7 0.0 copy-done.5
  25.8 0.6 copy-done.6
  26.4 0.1 copy-done.7
  26.5 0.0 copy-done.8
  26.5 8.3 %shard_map.101 = bf16[4,8,16,768]{3,2,1,0:T(8,128)(2,1)} custom-call(s32[1]{0:T(128)} %bitcast.me_ref.refs_0_, f32[2,8,1024]{2,1,0:T(8,128)} %constant.11.clone.refs_1_, bf16[8,1024,256]{2,1,0:T(8,128)(2,1)} %constant.12.clone.refs_2_, bf16[704,128]{1,0:T(8,128)(2,1)} %get-tuple-element.13.refs_3_, bf16[704,128]{1,0:T(8,128)(2,1)} %copy-done.2, ...), custom_call_target="tpu_custom_call" | custom-call | tf_op jit(solution)/shard_map/pallas_call | solution.py:214
  34.8 0.0 copy-start
  34.8 0.0 copy-start.1
  34.8 6.2 %all-to-all-start = ((bf16[32,16,768]{2,1,0:T(8,128)(2,1)}), bf16[32,16,768]{2,1,0:T(8,128)(2,1)S(1)}, u32[]{:S(2)}, u32[]{:S(2)}) async-start(bf16[32,16,768]{2,1,0:T(8,128)(2,1)} %bitcast.16), calls=%async_computation | async-start | bytes 1572864 | tf_op jit(solution)/shard_map/all_to_all | solution.py:305
  41.0 1.7 %copy.13 = bf16[1,768,2,512]{3,1,2,0:T(8,128)(2,1)S(1)} copy(bf16[1,768,2,512]{3,2,1,0:T(2,128)(2,1)} %param.16) | data formatting | bytes 3145728 | tf_op args[6]
  42.7 19.0 %all-to-all-done = bf16[32,16,768]{2,1,0:T(8,128)(2,1)S(1)} async-done(((bf16[32,16,768]{2,1,0:T(8,128)(2,1)}), bf16[32,16,768]{2,1,0:T(8,128)(2,1)S(1)}, u32[]{:S(2)}, u32[]{:S(2)}) %all-to-all-start) | async-done | bytes 786464 | tf_op jit(solution)/shard_map/all_to_all | solution.py:305
  61.6 0.0 copy-done
  61.6 0.0 copy-done.1
  61.6 1.3 %shard_map.102 = f32[32,8,128]{2,1,0:T(8,128)S(1)} custom-call(bf16[4,8,16,768]{3,2,1,0:T(8,128)(2,1)S(1)} %bitcast.14, f32[1,768]{1,0:T(1,128)S(1)} %bitcast.15, f32[64,64]{1,0:T(8,128)S(1)} %copy-done, bf16[2,768,512]{2,1,0:T(8,128)(2,1)S(1)} %bitcast.13), custom_call_target="tpu_custom_call" | custom-call | tf_op jit(solution)/shard_map/pallas_call | solution.py:214
  62.9 11.7 %all_to_all.10.part_ref = f32[32,8,128]{2,1,0:T(8,128)S(1)} all-to-all(f32[32,8,128]{2,1,0:T(8,128)S(1)} %shard_map.102), channel_id=1, replica_groups=mesh['patch'=4,'mode'=8] {'patch','mode'}, dimensions={0} | all-to-all | bytes 262144 | tf_op jit(solution)/shard_map/all_to_all | solution.py:324
  74.6 0.7 shard_map.103
Async XLA Ops:
  4.6 4.9 %collective-permute-start = (bf16[704,128]{1,0:T(8,128)(2,1)}, bf16[704,128]{1,0:T(8,128)(2,1)S(1)}, u32[]{:S(2)}, u32[]{:S(2)}) collective-permute-start(bf16[704,128]{1,0:T(8,128)(2,1)} %get-tuple-element.14), channel_id=1, source_target_pairs={{0,1},{1,0},{2,3},{3,2},{4,5},{5,4},{6,7},{7,6},{8,9},{9,8},{10,11... | collective-permute-start | bytes 540680 | tf_op jit(solution)/shard_map/ppermute | solution.py:281
  5.1 8.2 %collective-permute-start.1 = (bf16[704,128]{1,0:T(8,128)(2,1)}, bf16[704,128]{1,0:T(8,128)(2,1)S(1)}, u32[]{:S(2)}, u32[]{:S(2)}) collective-permute-start(bf16[704,128]{1,0:T(8,128)(2,1)} %get-tuple-element.15), channel_id=1, source_target_pairs={{0,2},{1,3},{2,0},{3,1},{4,6},{5,7},{6,4},{7,5},{8,10},{9,11},{10,... | collective-permute-start | bytes 540680 | tf_op jit(solution)/shard_map/ppermute | solution.py:281
  7.6 9.0 %collective-permute-start.2 = (bf16[704,128]{1,0:T(8,128)(2,1)}, bf16[704,128]{1,0:T(8,128)(2,1)S(1)}, u32[]{:S(2)}, u32[]{:S(2)}) collective-permute-start(bf16[704,128]{1,0:T(8,128)(2,1)} %get-tuple-element.16), channel_id=1, source_target_pairs={{0,3},{1,2},{2,1},{3,0},{4,7},{5,6},{6,5},{7,4},{8,11},{9,10},{10,... | collective-permute-start | bytes 540680 | tf_op jit(solution)/shard_map/ppermute | solution.py:281
  7.7 9.0 %collective-permute-start.3 = (bf16[704,128]{1,0:T(8,128)(2,1)}, bf16[704,128]{1,0:T(8,128)(2,1)S(1)}, u32[]{:S(2)}, u32[]{:S(2)}) collective-permute-start(bf16[704,128]{1,0:T(8,128)(2,1)} %get-tuple-element.17), channel_id=1, source_target_pairs={{0,4},{1,5},{2,6},{3,7},{4,0},{5,1},{6,2},{7,3},{8,12},{9,13},{10,... | collective-permute-start | bytes 540680 | tf_op jit(solution)/shard_map/ppermute | solution.py:281
  9.5 16.2 %collective-permute-start.4 = (bf16[704,128]{1,0:T(8,128)(2,1)}, bf16[704,128]{1,0:T(8,128)(2,1)S(1)}, u32[]{:S(2)}, u32[]{:S(2)}) collective-permute-start(bf16[704,128]{1,0:T(8,128)(2,1)} %get-tuple-element.18), channel_id=1, source_target_pairs={{0,5},{1,4},{2,7},{3,6},{4,1},{5,0},{6,3},{7,2},{8,13},{9,12},{10,... | collective-permute-start | bytes 540680 | tf_op jit(solution)/shard_map/ppermute | solution.py:281
  9.5 16.2 %copy-start.2 = (bf16[704,128]{1,0:T(8,128)(2,1)}, bf16[704,128]{1,0:T(8,128)(2,1)S(1)}, u32[]{:S(2)}) copy-start(bf16[704,128]{1,0:T(8,128)(2,1)S(1)} %collective-permute-done.refs_4_) | copy-start | bytes 540676
  9.5 16.2 %collective-permute-start.5 = (bf16[704,128]{1,0:T(8,128)(2,1)}, bf16[704,128]{1,0:T(8,128)(2,1)S(1)}, u32[]{:S(2)}, u32[]{:S(2)}) collective-permute-start(bf16[704,128]{1,0:T(8,128)(2,1)} %get-tuple-element.19), channel_id=1, source_target_pairs={{0,6},{1,7},{2,4},{3,5},{4,2},{5,3},{6,0},{7,1},{8,14},{9,15},{10,... | collective-permute-start | bytes 540680 | tf_op jit(solution)/shard_map/ppermute | solution.py:281
  13.3 12.5 %copy-start.3 = (bf16[704,128]{1,0:T(8,128)(2,1)}, bf16[704,128]{1,0:T(8,128)(2,1)S(1)}, u32[]{:S(2)}) copy-start(bf16[704,128]{1,0:T(8,128)(2,1)S(1)} %collective-permute-done.1.refs_5_) | copy-start | bytes 540676
  13.3 12.4 %collective-permute-start.6 = (bf16[704,128]{1,0:T(8,128)(2,1)}, bf16[704,128]{1,0:T(8,128)(2,1)S(1)}, u32[]{:S(2)}, u32[]{:S(2)}) collective-permute-start(bf16[704,128]{1,0:T(8,128)(2,1)} %get-tuple-element.20), channel_id=1, source_target_pairs={{0,7},{1,6},{2,5},{3,4},{4,3},{5,2},{6,1},{7,0},{8,15},{9,14},{10,... | collective-permute-start | bytes 540680 | tf_op jit(solution)/shard_map/ppermute | solution.py:281
  16.7 9.0 %copy-start.4 = (bf16[704,128]{1,0:T(8,128)(2,1)}, bf16[704,128]{1,0:T(8,128)(2,1)S(1)}, u32[]{:S(2)}) copy-start(bf16[704,128]{1,0:T(8,128)(2,1)S(1)} %collective-permute-done.2.refs_6_) | copy-start | bytes 540676
  16.7 9.0 %copy-start.5 = (bf16[704,128]{1,0:T(8,128)(2,1)}, bf16[704,128]{1,0:T(8,128)(2,1)S(1)}, u32[]{:S(2)}) copy-start(bf16[704,128]{1,0:T(8,128)(2,1)S(1)} %collective-permute-done.3.refs_7_) | copy-start | bytes 540676
  25.7 0.7 copy-start.6
  25.7 0.8 %copy-start.7 = (bf16[704,128]{1,0:T(8,128)(2,1)}, bf16[704,128]{1,0:T(8,128)(2,1)S(1)}, u32[]{:S(2)}) copy-start(bf16[704,128]{1,0:T(8,128)(2,1)S(1)} %collective-permute-done.5.refs_9_) | copy-start | bytes 540676
  25.7 0.8 %copy-start.8 = (bf16[704,128]{1,0:T(8,128)(2,1)}, bf16[704,128]{1,0:T(8,128)(2,1)S(1)}, u32[]{:S(2)}) copy-start(bf16[704,128]{1,0:T(8,128)(2,1)S(1)} %collective-permute-done.6.refs_10_) | copy-start | bytes 540676
  34.8 26.8 %copy-start = (f32[64,64]{1,0:T(8,128)S(1)}, f32[64,64]{1,0:T(8,128)}, u32[]{:S(2)}) copy-start(f32[64,64]{1,0:T(8,128)} %cov_ref.1) | copy-start | bytes 49156
  34.8 26.8 %copy-start.1 = (f32[768,1]{0,1:T(1,128)S(1)}, f32[768,1]{0,1:T(1,128)}, u32[]{:S(2)}) copy-start(f32[768,1]{0,1:T(1,128)} %param.14) | copy-start | bytes 9220
  34.8 26.8 %all-to-all-start = ((bf16[32,16,768]{2,1,0:T(8,128)(2,1)}), bf16[32,16,768]{2,1,0:T(8,128)(2,1)S(1)}, u32[]{:S(2)}, u32[]{:S(2)}) async-start(bf16[32,16,768]{2,1,0:T(8,128)(2,1)} %bitcast.16), calls=%async_computation | async-start | bytes 1572864 | tf_op jit(solution)/shard_map/all_to_all | solution.py:305

commit v3 on v2

v3 whole, which is shorter than its diff:
```python
import functools
import math

import jax
import jax.numpy as jnp
import ml_dtypes
import numpy as np
from jax import lax
from jax.experimental import pallas as pl
from jax.experimental.pallas import tpu as pltpu
from jax.sharding import PartitionSpec as P

LANES = 128
MIB = 1 << 20
HALVES = 2


def rotate(value, step, points):
    re, im = value
    step %= points
    if step == 0:
        return re, im
    if 2 * step == points:
        return -re, -im
    if 4 * step == points:
        return im, -re
    if 8 * step == points:
        return (re + im) * math.sqrt(0.5), (im - re) * math.sqrt(0.5)
    if 8 * step == 3 * points:
        return (im - re) * math.sqrt(0.5), (re + im) * -math.sqrt(0.5)
    c, s = math.cos(2 * math.pi * step / points), math.sin(2 * math.pi * step / points)
    return re * c + im * s, im * c - re * s


def dft(values):
    n = len(values)
    if n == 1:
        return values
    half = n // 2
    even, odd = dft(values[0::2]), dft(values[1::2])
    out = [None] * n
    for b in range(half):
        re, im = rotate(odd[b], b, n)
        out[b] = even[b][0] + re, even[b][1] + im
        out[b + half] = even[b][0] - re, even[b][1] - im
    return out


def whiten_kernel(half, with_leg, me_ref, after_ref, sky_hbm, mask_hbm, factor_hbm, leg_hbm, sort_hbm, *refs):
    sky, mask, factor, leg, sort, white, stage, sems = refs[-8:]
    outs = refs[:-8]
    cycles, chans, pixels = sky.shape
    groups = len(outs)
    part = white.shape[0] // cycles
    width = part // groups
    split = pixels // LANES
    sources, targets = (sky_hbm, mask_hbm, factor_hbm, sort_hbm), (sky, mask, factor, sort)
    if with_leg:
        sources, targets = sources + (leg_hbm,), targets + (leg,)
    copies = [pltpu.make_async_copy(a, b, sems.at[n]) for n, (a, b) in enumerate(zip(sources, targets))]
    for copy in copies:
        copy.start()
    for copy in copies[:3]:
        copy.wait()
    for r in range(cycles):
        rows = factor[r, half * part : (half + 1) * part, :]
        high = rows.astype(jnp.bfloat16)
        low = (rows - high.astype(jnp.float32)).astype(jnp.bfloat16)
        both = jnp.concatenate([high, low], axis=1)
        pair = jnp.concatenate([sky[r], sky[r]], axis=0)
        value = jnp.dot(both, pair, preferred_element_type=jnp.float32)
        value = value * mask[r : r + 1, :].astype(jnp.float32)
        white[r * part : (r + 1) * part, :] = value.astype(jnp.bfloat16)
    for copy in copies[3:]:
        copy.wait()
    start = split * cycles * width
    if with_leg:
        rows = jnp.concatenate([leg[r] for r in range(cycles)], axis=0).astype(jnp.bfloat16)
        count = rows.shape[0]
        for n in range(rows.shape[1] // LANES):
            for e in range(groups):
                stage[e, start + n * count : start + (n + 1) * count, :] = rows[:, n * LANES : (n + 1) * LANES]
    for pair in range(split // 2):
        wide = slice(pair * 2 * LANES, (pair + 1) * 2 * LANES)
        value = jnp.dot(white[...], sort[:, wide], preferred_element_type=jnp.float32)
        for side in range(2):
            s = pair * 2 + side
            block = value[:, side * LANES : (side + 1) * LANES]
            for e in range(groups):
                rows = [block[r * part + e * width : r * part + (e + 1) * width] for r in range(cycles)]
                rows = jnp.concatenate(rows, axis=0).astype(jnp.bfloat16)
                stage[e, s * cycles * width : (s + 1) * cycles * width, :] = rows
    me = me_ref[0]
    sends = [
        pltpu.make_async_copy(stage.at[jnp.bitwise_xor(me, n)], outs[n], sems.at[5 + n]) for n in range(groups)
    ]
    for send in sends:
        send.start()
    for send in sends:
        send.wait()


def modes_kernel(cycles, offsets, sources, own_leg, me_ref, after_ref, twiddle_ref, table_hbm, *refs):
    slots, legs = refs[:sources], refs[sources : 2 * sources]
    out_ref, table, left, leg, prod_a, prod_b, x_ref, table_sems = refs[2 * sources :]
    tiles = table.shape[0]
    split = twiddle_ref.shape[1]
    rows = left.shape[0]
    width = rows // (cycles * split)
    group = x_ref.shape[3] // width
    blocks = leg.shape[1] // (tiles * LANES)
    per = out_ref.shape[3] // LANES
    count = cycles * offsets
    me = me_ref[0]

    def copy(tile):
        return pltpu.make_async_copy(table_hbm.at[tile], table.at[tile], table_sems.at[tile])

    for tile in range(tiles):
        copy(tile).start()
    for slot in range(sources):
        q = jnp.bitwise_xor(me, slot)
        left[:, pl.ds(pl.multiple_of(q * LANES, LANES), LANES)] = slots[slot][:rows, :]
        for n in range(per):
            lanes = pl.ds(pl.multiple_of((q * per + n) * LANES, LANES), LANES)
            leg[:, lanes] = legs[slot][own_leg + n * count : own_leg + (n + 1) * count, :].astype(jnp.float32)

    def product(tile, prod):
        prod[...] = jnp.dot(left[...], table[tile], preferred_element_type=jnp.float32)

    def use(tile, prod):
        lanes = pl.ds(pl.multiple_of(tile * LANES, LANES), LANES)
        cosine, sine = twiddle_ref[0, :, lanes], twiddle_ref[1, :, lanes]
        tall = group * width
        place_in = lax.broadcasted_iota(jnp.int32, (tall, LANES), 0)
        for pack in range(cycles // group):
            values = []
            for s in range(split):
                place = (s * cycles + pack * group) * width
                re = prod[place : place + tall, :LANES]
                im = prod[place : place + tall, LANES:]
                if s == 0:
                    values.append((re, -im))
                else:
                    c, d = cosine[s : s + 1, :], sine[s : s + 1, :]
                    values.append((re * c - im * d, -(re * d) - im * c))
            parts = dft(values)
            for b in range(blocks):
                x_ref[b, 0, pack] = parts[b][0]
                x_ref[b, 1, pack] = parts[b][1]
        for b in range(blocks):
            mode_tile = b * tiles + tile
            d, n = mode_tile // per, mode_tile % per
            mode = pl.ds(pl.multiple_of(mode_tile * LANES, LANES), LANES)
            for k in range(offsets):
                total = [None, None]
                for pack in range(cycles // group):
                    row = None
                    for g in range(group):
                        r = pack * group + g
                        next_row = leg[r * offsets + k : r * offsets + k + 1, mode]
                        if g == 0:
                            row = jnp.broadcast_to(next_row, (tall, LANES))
                        else:
                            row = jnp.where(place_in < g * width, row, next_row)
                    for t in range(2):
                        term = row * x_ref[b, t, pack]
                        total[t] = term if pack == 0 else total[t] + term
                step = tall // 2
                while step >= width:
                    total = [value + pltpu.roll(value, step, 0) for value in total]
                    step //= 2
                if group == 1:
                    both = jnp.concatenate(total, axis=0)
                else:
                    both = jnp.where(place_in < width, total[0], total[1])[: 2 * width]
                place = pl.ds(pl.multiple_of(n * LANES, LANES), LANES)
                out_ref[k, d, :, place] = both.astype(jnp.bfloat16)

    copy(0).wait()
    product(0, prod_a)

    @pl.loop(0, tiles // 2)
    def _(step):
        copy(2 * step + 1).wait()

        @pl.when(2 * step + 2 < tiles)
        def _():
            copy(2 * step + 2).wait()

        product(2 * step + 1, prod_b)
        use(2 * step, prod_a)
        product(jnp.minimum(2 * step + 2, tiles - 1), prod_a)
        use(2 * step + 1, prod_b)


def sketch_kernel(band_ref, cov_ref, test_ref, *refs):
    out_ref, left_ref = refs[-2:]
    chans = cov_ref.shape[0]
    for half, alm_ref in enumerate(refs[:-2]):
        patches, groups, rows, lanes = alm_ref.shape
        width = rows // 2
        for g in range(groups):
            part = alm_ref[0, g].astype(jnp.float32)
            for p in range(1, patches):
                part += alm_ref[p, g].astype(jnp.float32)
            part = part * band_ref[...]
            place = (half * groups + g) * width
            for t in range(2):
                left_ref[t, place : place + width, :] = part[t * width : (t + 1) * width]
    sketch = None
    for t in range(2):
        term = lax.dot_general(
            test_ref[t],
            left_ref[t].astype(jnp.bfloat16),
            (((0,), (1,)), ((), ())),
            preferred_element_type=jnp.float32,
        )
        sketch = term if t == 0 else sketch + term
    mixed = lax.dot_general(
        sketch,
        cov_ref[...],
        (((1,), (1,)), ((), ())),
        precision=lax.Precision.HIGHEST,
        preferred_element_type=jnp.float32,
    )
    if out_ref.ndim == 2:
        out_ref[...] = mixed
    else:
        owners, block, _ = out_ref.shape
        fold = out_ref.shape[2] // chans
        mixed = mixed.reshape(owners, fold, block, chans)
        out_ref[...] = jnp.concatenate([mixed[:, n] for n in range(fold)], axis=-1)


def total_kernel(part_ref, out_ref):
    block, chans = part_ref.shape[1], out_ref.shape[1]
    total = jnp.sum(part_ref[...], axis=0)
    for n in range(part_ref.shape[2] // chans):
        out_ref[n * block : (n + 1) * block, :] = total[:, n * chans : (n + 1) * chans]


def call(kernel, shape, scratch, mib, spaces, *operands, out_space=pltpu.VMEM, cost=(0, 0)):
    return pl.pallas_call(
        kernel,
        out_shape=shape,
        in_specs=[pl.BlockSpec(memory_space=space) for space in spaces],
        out_specs=jax.tree.map(lambda _: pl.BlockSpec(memory_space=out_space), shape),
        scratch_shapes=scratch,
        compiler_params=pltpu.CompilerParams(vmem_limit_bytes=mib * MIB),
        cost_estimate=pl.CostEstimate(flops=cost[0], bytes_accessed=cost[1], transcendentals=0),
    )(*operands)


def transform_tables(split, cycle):
    half = cycle // split
    step = np.arange(split)[:, None] * np.arange(half)[None, :] % cycle
    angle = step * (2.0 * math.pi / cycle)
    twiddle = np.stack([np.cos(angle), np.sin(angle)]).astype(np.float32)
    step = np.arange(half)[:, None] * np.arange(half)[None, :] % half
    angle = (step * (2.0 * math.pi / half)).reshape(half, half // LANES, LANES)
    table = np.transpose(np.concatenate([np.cos(angle), np.sin(angle)], axis=2), (1, 0, 2))
    return twiddle, table.astype(ml_dtypes.bfloat16)


def sorting(pixels, split):
    place = np.arange(pixels) % split * (pixels // split) + np.arange(pixels) // split
    return (place[:, None] == np.arange(pixels)[None, :]).astype(ml_dtypes.bfloat16)


def local(sky_map, pixel_mask, noise_factor, cycle_legendre, band_power, channel_cov, test_matrix):
    cycles, pixels, chans = sky_map.shape
    modes, _ = band_power.shape
    offsets = cycle_legendre.shape[2]
    columns = test_matrix.shape[3]
    mode_count, patches = lax.axis_size("mode"), lax.axis_size("patch")
    part_chans = chans // HALVES
    width = part_chans // mode_count
    group = max(1, 8 // width)
    split = pixels // LANES
    rows = split * cycles * width
    legs = cycles * offsets * (modes // LANES)
    tiles = mode_count
    blocks = modes * mode_count // (tiles * LANES)
    everyone = ("patch", "mode")
    hbm, vmem, bf16, f32, shape = pl.ANY, pltpu.VMEM, jnp.bfloat16, jnp.float32, jax.ShapeDtypeStruct

    me = lax.axis_index("mode").astype(jnp.int32).reshape(1)
    twiddle, table = transform_tables(split, pixels * mode_count)
    twiddle, table = jnp.asarray(twiddle), jnp.asarray(table)
    sort = jnp.asarray(sorting(pixels, split))
    order = sorted(range(1, mode_count), key=lambda n: (n < 2, -(n // 2 & n // 4 & 1), n % 2))

    sky = jnp.transpose(sky_map, (0, 2, 1))
    slots = []
    for half in range(HALVES):
        extra = legs if half == 0 else 0
        messages = call(
            functools.partial(whiten_kernel, half, half == 0),
            [shape((rows + extra, LANES), bf16)] * mode_count,
            [
                vmem((cycles, chans, pixels), bf16),
                vmem((cycles, pixels), jnp.int32),
                vmem((cycles, chans, chans), f32),
                vmem((cycles, offsets, modes), f32),
                vmem((pixels, pixels), bf16),
                vmem((cycles * part_chans, pixels), bf16),
                vmem((mode_count, rows + extra, LANES), bf16),
                pltpu.SemaphoreType.DMA((5 + mode_count,)),
            ],
            56,
            [pltpu.SMEM] + [hbm] * 6,
            me,
            slots[0][0] if half else sky,
            sky,
            pixel_mask,
            noise_factor[:, 0],
            jnp.transpose(cycle_legendre, (0, 2, 1)),
            sort,
            out_space=hbm,
            cost=(2 * cycles * part_chans * pixels * (pixels + 2 * chans), 8 * MIB),
        )
        received = [messages[0]] + [None] * (mode_count - 1)
        for n in order:
            received[n] = lax.ppermute(messages[n], "mode", [(i, i ^ n) for i in range(mode_count)])
        slots.append(received)

    parts = []
    for half in range(HALVES):
        alm = call(
            functools.partial(modes_kernel, cycles, offsets, mode_count, rows),
            shape((offsets, mode_count, 2 * width, modes), bf16),
            [
                vmem((tiles, tiles * LANES, 2 * LANES), bf16),
                vmem((rows, tiles * LANES), bf16),
                vmem((cycles * offsets, mode_count * modes), f32),
                vmem((rows, 2 * LANES), f32),
                vmem((rows, 2 * LANES), f32),
                vmem((blocks, 2, cycles // group, group * width, LANES), f32),
                pltpu.SemaphoreType.DMA((tiles,)),
            ],
            40,
            [pltpu.SMEM, hbm, vmem, hbm] + [vmem] * (2 * mode_count),
            me,
            parts[0] if half else sky,
            twiddle,
            table,
            *slots[half],
            *slots[0],
            cost=(4 * rows * (tiles * LANES) ** 2 * 2, 8 * MIB),
        )
        parts.append(alm.reshape(patches * mode_count, 2 * width, modes))
    parts = [lax.all_to_all(alm, everyone, 0, 0, tiled=True) for alm in parts]
    parts = [alm.reshape(patches, mode_count, 2 * width, modes) for alm in parts]

    share = columns // (patches * mode_count)
    fold = LANES // chans
    packed = share % (8 * fold) == 0
    part = call(
        sketch_kernel,
        shape((patches * mode_count, share // fold, LANES) if packed else (columns, chans), f32),
        [vmem((2, chans, modes), f32)],
        24,
        [vmem] * (3 + HALVES),
        jnp.transpose(band_power),
        channel_cov,
        jnp.transpose(test_matrix[0], (1, 0, 2)),
        *parts,
    )
    if not packed:
        part = part.reshape(patches * mode_count, share, chans)
    part = lax.all_to_all(part, everyone, 0, 0, tiled=True)
    return jnp.transpose(call(total_kernel, shape((share, chans), f32), [], 16, [vmem], part))


def solution(mesh):
    return jax.shard_map(
        local,
        mesh=mesh,
        in_specs=(
            P("patch", "mode", None),
            P("patch", "mode"),
            P("patch", "mode", None, None),
            P("patch", "mode", None),
            P("mode", "patch"),
            P(),
            P("patch", "mode", None, None),
        ),
        out_specs=P(None, ("patch", "mode")),
        check_vma=False,
    )
```

time: 75.6 us -> 86.8 us (1.15)
  blocking collectives: 11.7 us -> 28.1 us
  waiting for transfers between devices: 30.8 us -> 21.3 us
  Pallas kernels: 14.8 us -> 17.6 us
  starting transfers between devices: 15.4 us -> 17.6 us
    all_to_all x0 -> x1, blocking collectives: none -> 17.5 us  [local(): parts = [lax.all_to_all(alm, everyone, 0, 0, tiled=True) for alm in parts]]
    all_to_all x1, waiting for transfers between devices: 19 us -> 11.5 us  [local(): parts = [lax.all_to_all(alm, everyone, 0, 0, tiled=True) for alm in parts]]
    ppermute x7 -> x14, starting transfers between devices: 9.25 us -> 14.8 us  [local(): lax.ppermute(messages[n], 'mode', [(i, i ^ n) for i in range(mode_count)])]
    all_to_all x1, starting transfers between devices: 6.17 us -> 2.73 us  [local(): parts = [lax.all_to_all(alm, everyone, 0, 0, tiled=True) for alm in parts]]
    pallas_call x4 -> x6, Pallas kernels: 14.8 us -> 17.6 us  [call(): pl.pallas_call(kernel, out_shape=shape, in_specs=[pl.BlockSpec(memory_spa...]
    ppermute x7 -> x14, waiting for transfers between devices: 11.9 us -> 9.83 us  [local(): lax.ppermute(messages[n], 'mode', [(i, i ^ n) for i in range(mode_count)])]
    all_to_all x1, blocking collectives: 11.7 us -> 10.6 us  [local(): part = lax.all_to_all(part, everyone, 0, 0, tiled=True)]
    unnamed x19 -> x25, local copies, waits for them, and re-layouts: 2.43 us -> 1.71 us
  transfers between devices with their start and end apart: 8 -> 15, of which waited for: 4 -> 3; matrix products, arithmetic and copies ran while one was open for 2% -> 2% of each run, Pallas kernels for 0% -> 9%
where the time goes in v3:
time: 86.8 us; the launch traced here: 86.5 us
  blocking collectives  28.1 us (32%)
  waiting for transfers between devices  21.3 us (25%)
  Pallas kernels  17.6 us (20%)
  starting transfers between devices  17.6 us (20%)
  local copies, waits for them, and re-layouts  1.71 us (2%)
    pallas_call x6, Pallas kernels, call(): pl.pallas_call(kernel, out_shape=shape, in_specs=[pl.BlockSpec(memory_spa...  17.6 us
    all_to_all x1, blocking collectives, local(): parts = [lax.all_to_all(alm, everyone, 0, 0, tiled=True) for alm in parts]  17.5 us
    ppermute x14, starting transfers between devices, local(): lax.ppermute(messages[n], 'mode', [(i, i ^ n) for i in range(mode_count)])  14.8 us
    all_to_all x1, waiting for transfers between devices, local(): parts = [lax.all_to_all(alm, everyone, 0, 0, tiled=True) for alm in parts]  11.5 us
    all_to_all x1, blocking collectives, local(): part = lax.all_to_all(part, everyone, 0, 0, tiled=True)  10.6 us
    ppermute x14, waiting for transfers between devices, local(): lax.ppermute(messages[n], 'mode', [(i, i ^ n) for i in range(mode_count)])  9.83 us
    all_to_all x1, starting transfers between devices, local(): parts = [lax.all_to_all(alm, everyone, 0, 0, tiled=True) for alm in parts]  2.73 us
  transfers between devices with their start and end apart: 15, of which 3 were waited for; matrix products, arithmetic and copies ran while one was open for 2% of the time, Pallas kernels for 9%

profile of v3, /device:TPU:0, one launch (start us, length us, event | category | flops | bytes accessed | tf_op | source)
XLA Modules:
  0.0 86.5 jit_solution(9442510742063426182)
XLA Ops:
  0.0 3.9 %shard_map.100 = (bf16[448,128]{1,0:T(8,128)(2,1)}, bf16[448,128]{1,0:T(8,128)(2,1)}, bf16[448,128]{1,0:T(8,128)(2,1)}, bf16[448,128]{1,0:T(8,128)(2,1)}, bf16[4...) custom-call(s32[1]{0:T(128)} %bitcast.3.me_ref, ...), custom_call_target="tpu_custom_call" | custom-call | flops 603979776 | bytes 8388608 | tf_op jit(solution)/shard_map/pallas_call | solution.py:244
  3.9 0.0 copy-start.11
  4.0 0.0 copy-start.10
  4.0 0.0 copy-start.9
  4.0 0.0 copy-start.8
  4.0 0.0 copy-start.7
  4.0 0.0 copy-start
  4.0 0.0 copy-start.1
  4.0 0.0 copy-start.6
  4.0 0.5 collective-permute-start
  4.5 2.6 %collective-permute-start.1 = (bf16[448,128]{1,0:T(8,128)(2,1)}, bf16[448,128]{1,0:T(8,128)(2,1)S(1)}, u32[]{:S(2)}, u32[]{:S(2)}) collective-permute-start(bf16[448,128]{1,0:T(8,128)(2,1)} %get-tuple-element.23), channel_id=1, source_target_pairs={{0,2},{1,3},{2,0},{3,1},{4,6},{5,7},{6,4},{7,5},{8,10},{9,11},{10,... | collective-permute-start | bytes 344072 | tf_op jit(solution)/shard_map/ppermute | solution.py:325
  7.1 3.7 %shard_map.102 = (bf16[256,128]{1,0:T(8,128)(2,1)}, bf16[256,128]{1,0:T(8,128)(2,1)}, bf16[256,128]{1,0:T(8,128)(2,1)}, bf16[256,128]{1,0:T(8,128)(2,1)}, bf16[2...) custom-call(s32[1]{0:T(128)} %bitcast.3.me_ref, ...), custom_call_target="tpu_custom_call" | custom-call | flops 603979776 | bytes 8388608 | tf_op jit(solution)/shard_map/pallas_call | solution.py:244
  10.8 1.6 %collective-permute-start.10 = (bf16[256,128]{1,0:T(8,128)(2,1)}, bf16[256,128]{1,0:T(8,128)(2,1)S(1)}, u32[]{:S(2)}, u32[]{:S(2)}) collective-permute-start(bf16[256,128]{1,0:T(8,128)(2,1)} %get-tuple-element.33), channel_id=1, source_target_pairs={{0,4},{1,5},{2,6},{3,7},{4,0},{5,1},{6,2},{7,3},{8,12},{9,13},{10,... | collective-permute-start | bytes 196616 | tf_op jit(solution)/shard_map/ppermute | solution.py:325
  12.4 0.0 collective-permute-start.11
  12.4 0.4 collective-permute-start.2
  12.8 2.5 %collective-permute-done.10.refs_4_ = bf16[256,128]{1,0:T(8,128)(2,1)S(1)} collective-permute-done((bf16[256,128]{1,0:T(8,128)(2,1)}, bf16[256,128]{1,0:T(8,128)(2,1)S(1)}, u32[]{:S(2)}, u32[]{:S(2)}) %collective-permute-start.10) | collective-permute-done | bytes 65568 | tf_op jit(solution)/shard_map/ppermute | solution.py:325
  15.3 2.2 %collective-permute-start.3 = (bf16[448,128]{1,0:T(8,128)(2,1)S(1)}, bf16[448,128]{1,0:T(8,128)(2,1)S(1)}, u32[]{:S(2)}, u32[]{:S(2)}) collective-permute-start(bf16[448,128]{1,0:T(8,128)(2,1)S(1)} %copy-done.10), channel_id=1, source_target_pairs={{0,4},{1,5},{2,6},{3,7},{4,0},{5,1},{6,2},{7,3},{8,12},{9,13},{10,... | collective-permute-start | bytes 344072 | tf_op jit(solution)/shard_map/ppermute | solution.py:325
  17.5 0.0 collective-permute-done.11.refs_5_
  17.5 0.4 collective-permute-start.4
  17.9 0.0 collective-permute-done.refs_1_.refs_9_
  17.9 0.9 collective-permute-start.5
  18.8 0.0 collective-permute-done.1.refs_2_.refs_10_
  18.8 1.2 %collective-permute-start.6 = (bf16[448,128]{1,0:T(8,128)(2,1)S(1)}, bf16[448,128]{1,0:T(8,128)(2,1)S(1)}, u32[]{:S(2)}, u32[]{:S(2)}) collective-permute-start(bf16[448,128]{1,0:T(8,128)(2,1)S(1)} %copy-done.7), channel_id=1, source_target_pairs={{0,7},{1,6},{2,5},{3,4},{4,3},{5,2},{6,1},{7,0},{8,15},{9,14},{10,... | collective-permute-start | bytes 344072 | tf_op jit(solution)/shard_map/ppermute | solution.py:325
  19.9 0.0 collective-permute-done.2.refs_3_.refs_11_
  19.9 1.9 %collective-permute-start.12 = (bf16[256,128]{1,0:T(8,128)(2,1)}, bf16[256,128]{1,0:T(8,128)(2,1)S(1)}, u32[]{:S(2)}, u32[]{:S(2)}) collective-permute-start(bf16[256,128]{1,0:T(8,128)(2,1)} %get-tuple-element.35), channel_id=1, source_target_pairs={{0,6},{1,7},{2,4},{3,5},{4,2},{5,3},{6,0},{7,1},{8,14},{9,15},{10,... | collective-permute-start | bytes 196616 | tf_op jit(solution)/shard_map/ppermute | solution.py:325
  21.8 0.0 collective-permute-done.3.refs_4_.refs_12_
  21.8 1.4 %collective-permute-start.13 = (bf16[256,128]{1,0:T(8,128)(2,1)}, bf16[256,128]{1,0:T(8,128)(2,1)S(1)}, u32[]{:S(2)}, u32[]{:S(2)}) collective-permute-start(bf16[256,128]{1,0:T(8,128)(2,1)} %get-tuple-element.36), channel_id=1, source_target_pairs={{0,7},{1,6},{2,5},{3,4},{4,3},{5,2},{6,1},{7,0},{8,15},{9,14},{10,... | collective-permute-start | bytes 196616 | tf_op jit(solution)/shard_map/ppermute | solution.py:325
  23.2 7.3 %collective-permute-done.4.refs_5_.refs_13_ = bf16[448,128]{1,0:T(8,128)(2,1)S(1)} collective-permute-done((bf16[448,128]{1,0:T(8,128)(2,1)S(1)}, bf16[448,128]{1,0:T(8,128)(2,1)S(1)}, u32[]{:S(2)}, u32[]{:S(2)}) %collective-permute-start.4) | collective-permute-done | bytes 114720 | tf_op jit(solution)/shard_map/ppermute | solution.py:325
  30.5 0.0 collective-permute-start.7
  30.5 0.0 collective-permute-done.5.refs_6_.refs_14_
  30.5 0.5 collective-permute-start.8
  31.0 0.0 collective-permute-done.6.refs_7_.refs_15_
  31.0 1.3 %collective-permute-start.9 = (bf16[256,128]{1,0:T(8,128)(2,1)}, bf16[256,128]{1,0:T(8,128)(2,1)S(1)}, u32[]{:S(2)}, u32[]{:S(2)}) collective-permute-start(bf16[256,128]{1,0:T(8,128)(2,1)} %get-tuple-element.32), channel_id=1, source_target_pairs={{0,3},{1,2},{2,1},{3,0},{4,7},{5,6},{6,5},{7,4},{8,11},{9,10},{10,... | collective-permute-start | bytes 196616 | tf_op jit(solution)/shard_map/ppermute | solution.py:325
  32.4 0.0 copy-done.1
  32.4 4.4 %shard_map.101 = bf16[4,8,8,768]{3,2,1,0:T(8,128)(2,1)} custom-call(s32[1]{0:T(128)} %bitcast.3.me_ref, bf16[8,64,1024]{2,1,0:T(8,128)(2,1)S(1)} %bitcast.18, f32[2,8,1024]{2,1,0:T(8,128)S(1)} %copy-done.6, bf16[8,1024,256]{2,1,0:T(8,128)(2,1)S(1)} %copy-done.5, bf16[448,128]{1,0:T(8,128)(2,1)S(1)} %copy-done.1, ...), custom_call_target="tpu_custom_call" | custom-call | flops 2147483648 | bytes 8388608 | tf_op jit(solution)/shard_map/pallas_call | solution.py:244
  36.7 0.0 collective-permute-done.12.refs_6_
  36.7 0.0 collective-permute-done.13.refs_7_
  36.8 0.0 collective-permute-done.7.refs_1_
  36.8 0.0 collective-permute-done.8.refs_2_
  36.8 0.0 collective-permute-done.9.refs_3_
  36.8 3.6 %shard_map.103 = bf16[4,8,8,768]{3,2,1,0:T(8,128)(2,1)S(1)} custom-call(s32[1]{0:T(128)} %bitcast.3.me_ref, bf16[32,8,768]{2,1,0:T(8,128)(2,1)} %bitcast.7.after_ref, f32[2,8,1024]{2,1,0:T(8,128)S(1)} %copy-done.6, bf16[8,1024,256]{2,1,0:T(8,128)(2,1)S(1)} %copy-done.5, bf16[256,128]{1,0:T(8,128)(2,1)S(1)} %copy-done.4, ...), custom_call_target="tpu_custom_call" | custom-call | flops 2147483648 | bytes 8388608 | tf_op jit(solution)/shard_map/pallas_call | solution.py:244
  40.4 17.5 %all_to_all.15 = bf16[32,8,768]{2,1,0:T(8,128)(2,1)S(1)} all-to-all(bf16[32,8,768]{2,1,0:T(8,128)(2,1)S(1)} %bitcast.22), channel_id=1, replica_groups=mesh['patch'=4,'mode'=8] {'patch','mode'}, dimensions={0} | all-to-all | bytes 786432 | tf_op jit(solution)/shard_map/all_to_all | solution.py:353
  58.0 2.7 %all-to-all-start = ((bf16[32,8,768]{2,1,0:T(8,128)(2,1)}), bf16[32,8,768]{2,1,0:T(8,128)(2,1)S(1)}, u32[]{:S(2)}, u32[]{:S(2)}) async-start(bf16[32,8,768]{2,1,0:T(8,128)(2,1)} %bitcast.7.after_ref), calls=%async_computation | async-start | bytes 786432 | tf_op jit(solution)/shard_map/all_to_all | solution.py:353
  60.7 1.7 %copy.13 = bf16[1,768,2,512]{3,1,2,0:T(8,128)(2,1)S(1)} copy(bf16[1,768,2,512]{3,2,1,0:T(2,128)(2,1)} %param.16) | data formatting | bytes 3145728 | tf_op args[6]
  62.4 11.5 %all-to-all-done = bf16[32,8,768]{2,1,0:T(8,128)(2,1)S(1)} async-done(((bf16[32,8,768]{2,1,0:T(8,128)(2,1)}), bf16[32,8,768]{2,1,0:T(8,128)(2,1)S(1)}, u32[]{:S(2)}, u32[]{:S(2)}) %all-to-all-start) | async-done | bytes 393248 | tf_op jit(solution)/shard_map/all_to_all | solution.py:353
  73.9 1.4 %shard_map.104 = f32[32,8,128]{2,1,0:T(8,128)S(1)} custom-call(f32[1,768]{1,0:T(1,128)S(1)} %bitcast.23, f32[64,64]{1,0:T(8,128)S(1)} %copy-done.2, bf16[2,768,512]{2,1,0:T(8,128)(2,1)S(1)} %bitcast.19, bf16[4,8,8,768]{3,2,1,0:T(8,128)(2,1)S(1)} %bitcast.21, bf16[4,8,8,768]{3,2,1,0:T(8,128)(2,1)S(1)} %bitcast.20), custom_call_target="tpu_custom_call" | custom-call | tf_op jit(solution)/shard_map/pallas_call | solution.py:244
  75.2 10.6 %all_to_all.16.part_ref = f32[32,8,128]{2,1,0:T(8,128)S(1)} all-to-all(f32[32,8,128]{2,1,0:T(8,128)S(1)} %shard_map.104), channel_id=1, replica_groups=mesh['patch'=4,'mode'=8] {'patch','mode'}, dimensions={0} | all-to-all | bytes 262144 | tf_op jit(solution)/shard_map/all_to_all | solution.py:372
  85.8 0.7 shard_map.105
  (15 shorter events, 0.0 us)
Async XLA Ops:
  0.0 32.4 %copy-start.5 = (bf16[8,1024,256]{2,1,0:T(8,128)(2,1)S(1)}, bf16[8,1024,256]{2,1,0:T(8,128)(2,1)}, u32[]{:S(2)}) copy-start(bf16[8,1024,256]{2,1,0:T(8,128)(2,1)} %constant.11.clone.table_hbm) | copy-start | bytes 12582916
  3.9 8.4 %copy-start.11 = (bf16[448,128]{1,0:T(8,128)(2,1)S(1)}, bf16[448,128]{1,0:T(8,128)(2,1)}, u32[]{:S(2)}) copy-start(bf16[448,128]{1,0:T(8,128)(2,1)} %get-tuple-element.24) | copy-start | bytes 344068
  4.0 11.4 %copy-start.10 = (bf16[448,128]{1,0:T(8,128)(2,1)S(1)}, bf16[448,128]{1,0:T(8,128)(2,1)}, u32[]{:S(2)}) copy-start(bf16[448,128]{1,0:T(8,128)(2,1)} %get-tuple-element.25) | copy-start | bytes 344068
  4.0 13.5 %copy-start.9 = (bf16[448,128]{1,0:T(8,128)(2,1)S(1)}, bf16[448,128]{1,0:T(8,128)(2,1)}, u32[]{:S(2)}) copy-start(bf16[448,128]{1,0:T(8,128)(2,1)} %get-tuple-element.26) | copy-start | bytes 344068
  4.0 13.9 %copy-start.8 = (bf16[448,128]{1,0:T(8,128)(2,1)S(1)}, bf16[448,128]{1,0:T(8,128)(2,1)}, u32[]{:S(2)}) copy-start(bf16[448,128]{1,0:T(8,128)(2,1)} %get-tuple-element.27) | copy-start | bytes 344068
  4.0 14.8 %copy-start.7 = (bf16[448,128]{1,0:T(8,128)(2,1)S(1)}, bf16[448,128]{1,0:T(8,128)(2,1)}, u32[]{:S(2)}) copy-start(bf16[448,128]{1,0:T(8,128)(2,1)} %get-tuple-element.28) | copy-start | bytes 344068
  4.0 28.4 %copy-start = (bf16[8,1024,64]{1,2,0:T(8,128)(2,1)S(1)}, bf16[8,1024,64]{1,2,0:T(8,128)(2,1)}, u32[]{:S(2)}) copy-start(bf16[8,1024,64]{1,2,0:T(8,128)(2,1)} %param.10) | copy-start | bytes 3145732
  4.0 28.4 %copy-start.1 = (bf16[448,128]{1,0:T(8,128)(2,1)S(1)}, bf16[448,128]{1,0:T(8,128)(2,1)}, u32[]{:S(2)}) copy-start(bf16[448,128]{1,0:T(8,128)(2,1)} %get-tuple-element.21.refs_0_.refs_8_.after_ref) | copy-start | bytes 344068
  4.0 28.4 %copy-start.6 = (f32[2,8,1024]{2,1,0:T(8,128)S(1)}, f32[2,8,1024]{2,1,0:T(8,128)}, u32[]{:S(2)}) copy-start(f32[2,8,1024]{2,1,0:T(8,128)} %constant.10.clone.twiddle_ref) | copy-start | bytes 196612
  4.0 13.9 %collective-permute-start = (bf16[448,128]{1,0:T(8,128)(2,1)}, bf16[448,128]{1,0:T(8,128)(2,1)S(1)}, u32[]{:S(2)}, u32[]{:S(2)}) collective-permute-start(bf16[448,128]{1,0:T(8,128)(2,1)} %get-tuple-element.22), channel_id=1, source_target_pairs={{0,1},{1,0},{2,3},{3,2},{4,5},{5,4},{6,7},{7,6},{8,9},{9,8},{10,11... | collective-permute-start | bytes 344072 | tf_op jit(solution)/shard_map/ppermute | solution.py:325
  4.5 14.2 %collective-permute-start.1 = (bf16[448,128]{1,0:T(8,128)(2,1)}, bf16[448,128]{1,0:T(8,128)(2,1)S(1)}, u32[]{:S(2)}, u32[]{:S(2)}) collective-permute-start(bf16[448,128]{1,0:T(8,128)(2,1)} %get-tuple-element.23), channel_id=1, source_target_pairs={{0,2},{1,3},{2,0},{3,1},{4,6},{5,7},{6,4},{7,5},{8,10},{9,11},{10,... | collective-permute-start | bytes 344072 | tf_op jit(solution)/shard_map/ppermute | solution.py:325
  10.8 4.5 %collective-permute-start.10 = (bf16[256,128]{1,0:T(8,128)(2,1)}, bf16[256,128]{1,0:T(8,128)(2,1)S(1)}, u32[]{:S(2)}, u32[]{:S(2)}) collective-permute-start(bf16[256,128]{1,0:T(8,128)(2,1)} %get-tuple-element.33), channel_id=1, source_target_pairs={{0,4},{1,5},{2,6},{3,7},{4,0},{5,1},{6,2},{7,3},{8,12},{9,13},{10,... | collective-permute-start | bytes 196616 | tf_op jit(solution)/shard_map/ppermute | solution.py:325
  12.4 5.1 %collective-permute-start.11 = (bf16[256,128]{1,0:T(8,128)(2,1)}, bf16[256,128]{1,0:T(8,128)(2,1)S(1)}, u32[]{:S(2)}, u32[]{:S(2)}) collective-permute-start(bf16[256,128]{1,0:T(8,128)(2,1)} %get-tuple-element.34), channel_id=1, source_target_pairs={{0,5},{1,4},{2,7},{3,6},{4,1},{5,0},{6,3},{7,2},{8,13},{9,12},{10,... | collective-permute-start | bytes 196616 | tf_op jit(solution)/shard_map/ppermute | solution.py:325
  12.4 7.5 %collective-permute-start.2 = (bf16[448,128]{1,0:T(8,128)(2,1)S(1)}, bf16[448,128]{1,0:T(8,128)(2,1)S(1)}, u32[]{:S(2)}, u32[]{:S(2)}) collective-permute-start(bf16[448,128]{1,0:T(8,128)(2,1)S(1)} %copy-done.11), channel_id=1, source_target_pairs={{0,3},{1,2},{2,1},{3,0},{4,7},{5,6},{6,5},{7,4},{8,11},{9,10},{10,... | collective-permute-start | bytes 344072 | tf_op jit(solution)/shard_map/ppermute | solution.py:325
  15.3 6.5 %collective-permute-start.3 = (bf16[448,128]{1,0:T(8,128)(2,1)S(1)}, bf16[448,128]{1,0:T(8,128)(2,1)S(1)}, u32[]{:S(2)}, u32[]{:S(2)}) collective-permute-start(bf16[448,128]{1,0:T(8,128)(2,1)S(1)} %copy-done.10), channel_id=1, source_target_pairs={{0,4},{1,5},{2,6},{3,7},{4,0},{5,1},{6,2},{7,3},{8,12},{9,13},{10,... | collective-permute-start | bytes 344072 | tf_op jit(solution)/shard_map/ppermute | solution.py:325
  17.5 13.0 %collective-permute-start.4 = (bf16[448,128]{1,0:T(8,128)(2,1)S(1)}, bf16[448,128]{1,0:T(8,128)(2,1)S(1)}, u32[]{:S(2)}, u32[]{:S(2)}) collective-permute-start(bf16[448,128]{1,0:T(8,128)(2,1)S(1)} %copy-done.9), channel_id=1, source_target_pairs={{0,5},{1,4},{2,7},{3,6},{4,1},{5,0},{6,3},{7,2},{8,13},{9,12},{10,... | collective-permute-start | bytes 344072 | tf_op jit(solution)/shard_map/ppermute | solution.py:325
  17.9 12.6 %collective-permute-start.5 = (bf16[448,128]{1,0:T(8,128)(2,1)S(1)}, bf16[448,128]{1,0:T(8,128)(2,1)S(1)}, u32[]{:S(2)}, u32[]{:S(2)}) collective-permute-start(bf16[448,128]{1,0:T(8,128)(2,1)S(1)} %copy-done.8), channel_id=1, source_target_pairs={{0,6},{1,7},{2,4},{3,5},{4,2},{5,3},{6,0},{7,1},{8,14},{9,15},{10,... | collective-permute-start | bytes 344072 | tf_op jit(solution)/shard_map/ppermute | solution.py:325
  18.8 12.3 %collective-permute-start.6 = (bf16[448,128]{1,0:T(8,128)(2,1)S(1)}, bf16[448,128]{1,0:T(8,128)(2,1)S(1)}, u32[]{:S(2)}, u32[]{:S(2)}) collective-permute-start(bf16[448,128]{1,0:T(8,128)(2,1)S(1)} %copy-done.7), channel_id=1, source_target_pairs={{0,7},{1,6},{2,5},{3,4},{4,3},{5,2},{6,1},{7,0},{8,15},{9,14},{10,... | collective-permute-start | bytes 344072 | tf_op jit(solution)/shard_map/ppermute | solution.py:325
  19.9 16.8 %collective-permute-start.12 = (bf16[256,128]{1,0:T(8,128)(2,1)}, bf16[256,128]{1,0:T(8,128)(2,1)S(1)}, u32[]{:S(2)}, u32[]{:S(2)}) collective-permute-start(bf16[256,128]{1,0:T(8,128)(2,1)} %get-tuple-element.35), channel_id=1, source_target_pairs={{0,6},{1,7},{2,4},{3,5},{4,2},{5,3},{6,0},{7,1},{8,14},{9,15},{10,... | collective-permute-start | bytes 196616 | tf_op jit(solution)/shard_map/ppermute | solution.py:325
  21.8 14.9 %collective-permute-start.13 = (bf16[256,128]{1,0:T(8,128)(2,1)}, bf16[256,128]{1,0:T(8,128)(2,1)S(1)}, u32[]{:S(2)}, u32[]{:S(2)}) collective-permute-start(bf16[256,128]{1,0:T(8,128)(2,1)} %get-tuple-element.36), channel_id=1, source_target_pairs={{0,7},{1,6},{2,5},{3,4},{4,3},{5,2},{6,1},{7,0},{8,15},{9,14},{10,... | collective-permute-start | bytes 196616 | tf_op jit(solution)/shard_map/ppermute | solution.py:325
  30.5 6.3 %collective-permute-start.7 = (bf16[256,128]{1,0:T(8,128)(2,1)}, bf16[256,128]{1,0:T(8,128)(2,1)S(1)}, u32[]{:S(2)}, u32[]{:S(2)}) collective-permute-start(bf16[256,128]{1,0:T(8,128)(2,1)} %get-tuple-element.30), channel_id=1, source_target_pairs={{0,1},{1,0},{2,3},{3,2},{4,5},{5,4},{6,7},{7,6},{8,9},{9,8},{10,11... | collective-permute-start | bytes 196616 | tf_op jit(solution)/shard_map/ppermute | solution.py:325
  30.5 6.3 %collective-permute-start.8 = (bf16[256,128]{1,0:T(8,128)(2,1)}, bf16[256,128]{1,0:T(8,128)(2,1)S(1)}, u32[]{:S(2)}, u32[]{:S(2)}) collective-permute-start(bf16[256,128]{1,0:T(8,128)(2,1)} %get-tuple-element.31), channel_id=1, source_target_pairs={{0,2},{1,3},{2,0},{3,1},{4,6},{5,7},{6,4},{7,5},{8,10},{9,11},{10,... | collective-permute-start | bytes 196616 | tf_op jit(solution)/shard_map/ppermute | solution.py:325
  31.0 5.8 %copy-start.4 = (bf16[256,128]{1,0:T(8,128)(2,1)S(1)}, bf16[256,128]{1,0:T(8,128)(2,1)}, u32[]{:S(2)}) copy-start(bf16[256,128]{1,0:T(8,128)(2,1)} %get-tuple-element.29.refs_0_) | copy-start | bytes 196612
  31.0 5.7 %collective-permute-start.9 = (bf16[256,128]{1,0:T(8,128)(2,1)}, bf16[256,128]{1,0:T(8,128)(2,1)S(1)}, u32[]{:S(2)}, u32[]{:S(2)}) collective-permute-start(bf16[256,128]{1,0:T(8,128)(2,1)} %get-tuple-element.32), channel_id=1, source_target_pairs={{0,3},{1,2},{2,1},{3,0},{4,7},{5,6},{6,5},{7,4},{8,11},{9,10},{10,... | collective-permute-start | bytes 196616 | tf_op jit(solution)/shard_map/ppermute | solution.py:325
  58.0 15.9 %copy-start.2 = (f32[64,64]{1,0:T(8,128)S(1)}, f32[64,64]{1,0:T(8,128)}, u32[]{:S(2)}) copy-start(f32[64,64]{1,0:T(8,128)} %cov_ref.1) | copy-start | bytes 49156
  58.0 15.9 %copy-start.3 = (f32[768,1]{0,1:T(1,128)S(1)}, f32[768,1]{0,1:T(1,128)}, u32[]{:S(2)}) copy-start(f32[768,1]{0,1:T(1,128)} %param.14) | copy-start | bytes 9220
  58.0 15.9 %all-to-all-start = ((bf16[32,8,768]{2,1,0:T(8,128)(2,1)}), bf16[32,8,768]{2,1,0:T(8,128)(2,1)S(1)}, u32[]{:S(2)}, u32[]{:S(2)}) async-start(bf16[32,8,768]{2,1,0:T(8,128)(2,1)} %bitcast.7.after_ref), calls=%async_computation | async-start | bytes 786432 | tf_op jit(solution)/shard_map/all_to_all | solution.py:353
